TPU v7x, 512 devices: a whole 4x8x8 slice. The times are simulated.
512 devices in a mesh: row: 32 (over x, y_lo, core), col: 16 (over y_hi, z).
Axes of the slice: x: 4, y: 8 (y_hi: 2, y_lo: 4; y = y_hi * 4 + y_lo), z: 8, core: 2. Of those that a mesh axis runs over, the one named last changes fastest.
Arguments:
- covariance: bfloat16 [24576, 24576], P('row', 'col'), as said below
Outputs:
- trailing: bfloat16 [24576, 24576], P('row', 'col')
Inputs may be any that keep to these rules, and one draw needn't show every extreme that they name: covariance is symmetric, and its leading 3 * 256 rows and columns form a positive definite block.
All inputs are finite; a program needn't handle non-finite values.
Results may differ from a plain program's by a relative error of at most 0.0058.
Values may be sent and summed in bfloat16 or wider, within the bound.
No kernel may reach another device: no remote copies, remote signals or barrier semaphores. Data moves between devices by JAX's collectives and lax.ppermute only.
A program may use at most 64 MiB of HBM per device.

v0:
```python
import jax
import jax.numpy as jnp
from jax import lax
from jax.sharding import PartitionSpec as P

NB = 256
ITERS = 3


def from_root(block, axis, owner):
    block = jnp.where(lax.axis_index(axis) == owner, block, jnp.zeros_like(block))
    return lax.psum(block, axis)


def per_device(covariance):
    rows_dev, cols_dev = covariance.shape
    n_rows = lax.axis_size("row")
    n_cols = lax.axis_size("col")
    row_ratio = n_rows // n_cols
    row_pos = lax.axis_index("row")
    col_pos = lax.axis_index("col")
    local_rows = row_pos * rows_dev + jnp.arange(rows_dev, dtype=jnp.int32)
    local_cols = col_pos * cols_dev + jnp.arange(cols_dev, dtype=jnp.int32)
    identity = jnp.eye(NB, dtype=jnp.float32)
    current = covariance
    for iteration in range(ITERS):
        first_col = iteration * NB
        owner_col = first_col // cols_dev
        col_offset = first_col % cols_dev
        owner_row = first_col // rows_dev
        row_offset = first_col % rows_dev
        panel_local = current[:, col_offset : col_offset + NB]
        panel_rows = from_root(panel_local, "col", owner_col)
        diag_block = from_root(panel_rows[row_offset : row_offset + NB], "row", owner_row)
        factor = jnp.linalg.cholesky(diag_block.astype(jnp.float32))
        inverse = jax.scipy.linalg.solve_triangular(factor, identity, lower=True)
        solved = jnp.dot(panel_rows.astype(jnp.float32), inverse.T, precision=lax.Precision.HIGHEST)
        row_factor = jnp.where((local_rows >= first_col)[:, None], solved, jnp.float32(0.0)).astype(
            jnp.bfloat16
        )
        pieces = []
        for member in range(row_ratio):
            source = col_pos * row_ratio + member
            pieces.append(from_root(row_factor, "row", source))
        col_factor = jnp.concatenate(pieces, axis=0)
        product = lax.dot_general(
            row_factor, col_factor, (((1,), (1,)), ((), ())), preferred_element_type=jnp.float32
        )
        current = (current.astype(jnp.float32) - product).astype(jnp.bfloat16)
    done = ITERS * NB
    trailing_mask = (local_rows >= done)[:, None] & (local_cols >= done)[None, :]
    return jnp.where(trailing_mask, current, jnp.zeros_like(current))


def solution(mesh):
    in_specs = (P("row", "col"),)
    out_specs = P("row", "col")
    return jax.shard_map(
        per_device, mesh=mesh, in_specs=in_specs, out_specs=out_specs, check_vma=False
    )
```

profile of v0, /device:TPU:1, one launch (start us, length us, event | category | flops | bytes accessed | tf_op | source)
XLA Modules:
  0.0 2444.2 jit_solution(10965992412238784697)
XLA Ops:
  6.5 2.8 copy.2
  10.3 191.3 %all-reduce.14.cloned.1.call-done = bf16[768,256]{0,1:T(8,128)(2,1)} async-done(((bf16[768,256]{0,1:T(8,128)(2,1)}), bf16[768,256]{0,1:T(8,128)(2,1)}) %all-reduce.14.cloned.1.call-update) | async-done | bytes 393232 | tf_op jit(solution)/shard_map/psum | solution.py:12
  201.6 1.6 slice_select_fusion.5
  203.3 266.6 %all-reduce.16.cloned.1.call-done = bf16[256,256]{0,1:T(8,128)(2,1)} async-done(((bf16[256,256]{0,1:T(8,128)(2,1)}), bf16[256,256]{0,1:T(8,128)(2,1)}) %all-reduce.16.cloned.1.call-update) | async-done | bytes 131088 | tf_op jit(solution)/shard_map/psum | solution.py:12
  470.0 1.0 copy.4
  471.0 0.9 fusion.23
  471.9 11.7 cholesky.172
  483.7 9.8 custom-call.15
  494.0 11.7 cholesky.189
  507.8 4.2 while.6
  508.7 1.3 bitcast_dynamic-update-slice_fusion.6
  510.7 1.3 bitcast_dynamic-update-slice_fusion.6
  512.0 19.7 custom-call.16
  532.6 2.4 broadcast_select_fusion.5
  535.1 283.5 %all-reduce.30.cloned.1.call-done = (bf16[768,256]{0,1:T(8,128)(2,1)}, bf16[768,256]{0,1:T(8,128)(2,1)}) async-done(((bf16[768,256]{0,1:T(8,128)(2,1)}, bf16[768,256]{0,1:T(8,128)(2,1)}), (bf16[768,256]{0,1:T(8,128)(2,1)}, bf16[768,256]{0,1:T(8,128)(2,1)})) %all-reduce.30.cloned.1.call-update) | async-done | bytes 786448 | tf_op jit(solution)/shard_map/psum | solution.py:12
  818.6 2.7 subtract_convert_fusion.2
  822.2 185.1 %all-reduce.18.cloned.1.call-done = bf16[768,256]{0,1:T(8,128)(2,1)} async-done(((bf16[768,256]{0,1:T(8,128)(2,1)}), bf16[768,256]{0,1:T(8,128)(2,1)}) %all-reduce.18.cloned.1.call-update) | async-done | bytes 393232 | tf_op jit(solution)/shard_map/psum | solution.py:12
  1007.2 1.6 slice_select_fusion.4
  1008.9 266.3 %all-reduce.20.cloned.1.call-done = bf16[256,256]{0,1:T(8,128)(2,1)} async-done(((bf16[256,256]{0,1:T(8,128)(2,1)}), bf16[256,256]{0,1:T(8,128)(2,1)}) %all-reduce.20.cloned.1.call-update) | async-done | bytes 131088 | tf_op jit(solution)/shard_map/psum | solution.py:12
  1275.2 1.0 copy.7
  1276.2 0.9 fusion.22
  1277.1 11.7 cholesky.206
  1288.9 9.8 custom-call.17
  1299.2 11.7 cholesky.223
  1313.6 4.2 while.7
  1314.4 1.4 bitcast_dynamic-update-slice_fusion.7
  1316.4 1.4 bitcast_dynamic-update-slice_fusion.7
  1317.8 19.7 custom-call.18
  1338.4 1.4 broadcast_select_fusion.4
  1339.8 283.4 %all-reduce.28.cloned.1.call-done = (bf16[768,256]{0,1:T(8,128)(2,1)}, bf16[768,256]{0,1:T(8,128)(2,1)}) async-done(((bf16[768,256]{0,1:T(8,128)(2,1)}, bf16[768,256]{0,1:T(8,128)(2,1)}), (bf16[768,256]{0,1:T(8,128)(2,1)}, bf16[768,256]{0,1:T(8,128)(2,1)})) %all-reduce.28.cloned.1.call-update) | async-done | bytes 786448 | tf_op jit(solution)/shard_map/psum | solution.py:12
  1623.3 1.9 subtract_convert_fusion.1
  1625.2 1.4 copy-done.1
  1627.5 185.1 %all-reduce.22.cloned.1.call-done = bf16[768,256]{0,1:T(8,128)(2,1)} async-done(((bf16[768,256]{0,1:T(8,128)(2,1)}), bf16[768,256]{0,1:T(8,128)(2,1)}) %all-reduce.22.cloned.1.call-update) | async-done | bytes 393232 | tf_op jit(solution)/shard_map/psum | solution.py:12
  1812.6 1.6 slice_select_fusion.3
  1814.3 266.7 %all-reduce.24.cloned.1.call-done = bf16[256,256]{0,1:T(8,128)(2,1)} async-done(((bf16[256,256]{0,1:T(8,128)(2,1)}), bf16[256,256]{0,1:T(8,128)(2,1)}) %all-reduce.24.cloned.1.call-update) | async-done | bytes 131088 | tf_op jit(solution)/shard_map/psum | solution.py:12
  2080.9 1.0 copy.10
  2081.9 1.0 fusion.21
  2082.9 11.7 cholesky.240
  2094.7 9.8 custom-call.19
  2105.0 11.7 cholesky.257
  2119.4 4.3 while.8
  2120.4 1.3 bitcast_dynamic-update-slice_fusion.8
  2122.4 1.3 bitcast_dynamic-update-slice_fusion.8
  2123.7 19.7 custom-call.20
  2144.3 1.4 broadcast_select_fusion.3
  2145.7 283.5 %all-reduce.26.cloned.1.call-done = (bf16[768,256]{0,1:T(8,128)(2,1)}, bf16[768,256]{0,1:T(8,128)(2,1)}) async-done(((bf16[768,256]{0,1:T(8,128)(2,1)}, bf16[768,256]{0,1:T(8,128)(2,1)}), (bf16[768,256]{0,1:T(8,128)(2,1)}, bf16[768,256]{0,1:T(8,128)(2,1)})) %all-reduce.26.cloned.1.call-update) | async-done | bytes 786448 | tf_op jit(solution)/shard_map/psum | solution.py:12
  2429.2 3.7 and_select_fusion
  2432.9 4.3 copy.13
  (88 shorter events, 14.7 us)
Async XLA Ops:
  6.5 195.1 %all-reduce.14.cloned.1.call-start = ((), (), s32[]{:S(2)}) async-start(), calls=%async_computation | async-start | bytes 786432 | tf_op jit(solution)/shard_map/psum | solution.py:12
  9.4 498.4 %copy-start = (bf16[768,1536]{0,1:T(8,128)(2,1)}, bf16[768,1536]{0,1:T(8,128)(2,1)S(1)}, u32[]{:S(2)}) copy-start(bf16[768,1536]{0,1:T(8,128)(2,1)S(1)} %copy.2) | copy-start | bytes 7077892
  10.2 459.7 %all-reduce.16.cloned.1.call-start = ((), (), s32[]{:S(2)}) async-start(), calls=%async_computation.1 | async-start | bytes 262144 | tf_op jit(solution)/shard_map/psum | solution.py:12
  203.2 615.4 %all-reduce.30.cloned.1.call-start = ((), (), s32[]{:S(2)}) async-start(), calls=%async_computation.8 | async-start | bytes 1572864 | tf_op jit(solution)/shard_map/psum | solution.py:12
  535.0 472.2 %all-reduce.18.cloned.1.call-start = ((), (), s32[]{:S(2)}) async-start(), calls=%async_computation.2 | async-start | bytes 786432 | tf_op jit(solution)/shard_map/psum | solution.py:12
  822.1 453.0 %all-reduce.20.cloned.1.call-start = ((), (), s32[]{:S(2)}) async-start(), calls=%async_computation.3 | async-start | bytes 262144 | tf_op jit(solution)/shard_map/psum | solution.py:12
  1008.8 614.4 %all-reduce.28.cloned.1.call-start = ((), (), s32[]{:S(2)}) async-start(), calls=%async_computation.7 | async-start | bytes 1572864 | tf_op jit(solution)/shard_map/psum | solution.py:12
  1310.9 27.5 %copy-start.4 = (bf16[768,256]{0,1:T(8,128)(2,1)S(1)}, bf16[768,256]{0,1:T(8,128)(2,1)}, u32[]{:S(2)}) copy-start(bf16[768,256]{0,1:T(8,128)(2,1)} %all-reduce.18.cloned.1.call-done) | copy-start | bytes 1179652
  1339.8 472.8 %all-reduce.22.cloned.1.call-start = ((), (), s32[]{:S(2)}) async-start(), calls=%async_computation.4 | async-start | bytes 786432 | tf_op jit(solution)/shard_map/psum | solution.py:12
  1625.2 1.4 copy-start.1
  1627.4 453.5 %all-reduce.24.cloned.1.call-start = ((), (), s32[]{:S(2)}) async-start(), calls=%async_computation.5 | async-start | bytes 262144 | tf_op jit(solution)/shard_map/psum | solution.py:12
  1814.2 615.0 %all-reduce.26.cloned.1.call-start = ((), (), s32[]{:S(2)}) async-start(), calls=%async_computation.6 | async-start | bytes 1572864 | tf_op jit(solution)/shard_map/psum | solution.py:12
  2081.9 62.4 %copy-start.3 = (bf16[768,256]{0,1:T(8,128)(2,1)S(1)}, bf16[768,256]{0,1:T(8,128)(2,1)}, u32[]{:S(2)}) copy-start(bf16[768,256]{0,1:T(8,128)(2,1)} %all-reduce.22.cloned.1.call-done) | copy-start | bytes 1179652
  2119.4 309.8 %copy-start.2 = (bf16[768,1536]{0,1:T(8,128)(2,1)S(1)}, bf16[768,1536]{0,1:T(8,128)(2,1)}, u32[]{:S(2)}) copy-start(bf16[768,1536]{0,1:T(8,128)(2,1)} %copy-done.1) | copy-start | bytes 7077892
Sparse Core Ops, SparseCore 0:
  10.4 191.2 all-reduce.13
  204.8 265.1 all-reduce.15
  535.1 283.4 all-reduce.29
  822.3 184.9 all-reduce.17
  1010.0 265.1 all-reduce.19
  1339.9 283.3 all-reduce.27
  1627.5 185.0 all-reduce.21
  1815.8 265.1 all-reduce.23
  2145.8 283.3 all-reduce.25
where the time goes:
time: 2450 us; the launch traced here: 2440 us
  waiting for transfers between devices  2210 us (90%)
  other arithmetic  172 us (7%)
    psum x9, waiting for transfers between devices, from_root(): return lax.psum(block, axis)  2210 us
    another operation x20, other arithmetic, per_device(): factor = jnp.linalg.cholesky(diag_block.astype(jnp.float32))  103 us
    another operation x7, other arithmetic, per_device(): inverse = jax.scipy.linalg.solve_triangular(factor, identity, lower=True)  59.1 us
  transfers between devices with their start and end apart: 9, of which 9 were waited for; matrix products, arithmetic and copies ran while one was open for 0% of the time, Pallas kernels for 0%

commit v1 on v0

v1 whole, which is shorter than its diff:
```python
import jax
import jax.numpy as jnp
from jax import lax
from jax.experimental import pallas as pl
from jax.experimental.pallas import tpu as pltpu
from jax.sharding import PartitionSpec as P

N = 768
B = 128
STEPS = N // B
HI = lax.Precision.HIGHEST


def mm(a, b):
    return jnp.dot(a, b, precision=HI, preferred_element_type=jnp.float32)


def mm_t(a, b):
    return lax.dot_general(
        a, b, (((0,), (0,)), ((), ())), precision=HI, preferred_element_type=jnp.float32
    )


def invert_factor(block):
    groups = B // 8
    lane = lax.broadcasted_iota(jnp.int32, (8, B), 1)
    sub = lax.broadcasted_iota(jnp.int32, (8, B), 0)
    left = [block[8 * g : 8 * g + 8] for g in range(groups)]
    right = [jnp.where(lane == sub + 8 * g, 1.0, 0.0).astype(jnp.float32) for g in range(groups)]
    done = []

    def over_rows(x, i):
        return jnp.broadcast_to(x[i : i + 1], (8, B))

    def over_lanes(x, i):
        return jnp.broadcast_to(x[:, i : i + 1], (8, B))

    for g in range(groups):
        first = 8 * g
        last = g == groups - 1
        row_l, row_r = left[g], right[g]
        own = [over_lanes(row_l, first + i) for i in range(8)]
        if not last:
            nxt_l, nxt_r = left[g + 1], right[g + 1]
            nxt = [over_lanes(nxt_l, first + i) for i in range(8)]
        pivot = jnp.ones((8, B), jnp.float32)
        for i in range(8):
            d = over_rows(own[i], i)
            r = 1.0 / d
            pivot = jnp.where(sub == i, d, pivot)
            m = jnp.where(sub > i, own[i] * r, 0.0)
            rows = [over_rows(own[t], i) for t in range(i + 1, 8)]
            for t in range(i + 1, 8):
                own[t] = own[t] - m * rows[t - i - 1]
            rl, rr = over_rows(row_l, i), over_rows(row_r, i)
            row_l = row_l - m * rl
            row_r = row_r - m * rr
            if not last:
                n = nxt[i] * r
                for t in range(i + 1, 8):
                    nxt[t] = nxt[t] - n * rows[t - i - 1]
                nxt_l = nxt_l - n * rl
                nxt_r = nxt_r - n * rr
        scale = lax.rsqrt(pivot)
        done.append(row_r * scale)
        if not last:
            left[g + 1], right[g + 1] = nxt_l, nxt_r
        if g + 2 < groups:
            ul = row_l * scale
            cut = jnp.where(lane >= first + 16, ul, 0.0)
            both = mm_t(cut, jnp.concatenate([ul, row_r * scale], axis=1))
            for q in range(g + 2, groups):
                left[q] = left[q] - both[8 * q : 8 * q + 8, :B]
                right[q] = right[q] - both[8 * q : 8 * q + 8, B:]
    return jnp.concatenate(done, axis=0)


def chol_kernel(a_ref, hi_ref, lo_ref, s_ref, w_ref):
    s_ref[...] = a_ref[...].astype(jnp.float32)
    w_ref[...] = jnp.zeros_like(w_ref)
    for k in range(STEPS):
        lo, hi = k * B, (k + 1) * B
        inv = invert_factor(s_ref[lo:hi, lo:hi])
        w_ref[lo:hi, lo:hi] = inv
        if k:
            w_ref[lo:hi, :lo] = mm(inv, w_ref[lo:hi, :lo])
        if hi < N:
            u = mm(inv, s_ref[lo:hi, hi:])
            for q in range(k + 1, STEPS):
                a, b = q * B, (q + 1) * B
                uq = u[:, a - hi : b - hi]
                s_ref[a:b, a:] = s_ref[a:b, a:] - mm_t(uq, u[:, a - hi :])
                w_ref[a:b, :hi] = w_ref[a:b, :hi] - mm_t(uq, w_ref[lo:hi, :hi])
    w = w_ref[...]
    high = w.astype(jnp.bfloat16)
    hi_ref[...] = high
    lo_ref[...] = (w - high.astype(jnp.float32)).astype(jnp.bfloat16)


def chol(a):
    vm = pl.BlockSpec(memory_space=pltpu.VMEM)
    return pl.pallas_call(
        chol_kernel,
        out_shape=[jax.ShapeDtypeStruct((N, N), jnp.bfloat16)] * 2,
        in_specs=[vm],
        out_specs=[vm, vm],
        scratch_shapes=[pltpu.VMEM((N, N), jnp.float32), pltpu.VMEM((N, N), jnp.float32)],
        compiler_params=pltpu.CompilerParams(vmem_limit_bytes=16 << 20),
        cost_estimate=pl.CostEstimate(flops=48_000_000_000, bytes_accessed=4_000_000, transcendentals=0),
        name="factor",
    )(a)


TILE = 256
PANEL = 256


def update_kernel(where_ref, cov_ref, rows_ref, mine_ref, other_ref, hi_ref, lo_ref, out_ref, left_ref):
    row, col, core = where_ref[0], where_ref[1], where_ref[2]
    step = pl.program_id(0)

    @pl.when(step == 0)
    def _():
        for k in range(N // PANEL):
            lo, hi = k * PANEL, (k + 1) * PANEL
            part = jnp.zeros((rows_ref.shape[0], PANEL), jnp.float32)
            for w_ref in (hi_ref, lo_ref):
                part += lax.dot_general(
                    rows_ref[:, :hi],
                    w_ref[lo:hi, :hi],
                    (((1,), (1,)), ((), ())),
                    preferred_element_type=jnp.float32,
                )
            left_ref[:, lo:hi] = part.astype(jnp.bfloat16)

    half = lax.div(step, N // TILE)
    at = pl.multiple_of(lax.rem(step, N // TILE) * TILE, TILE)
    panel = jnp.where(half == core, mine_ref[:, pl.ds(at, TILE)], other_ref[:, pl.ds(at, TILE)])
    parts = []
    for k in range(N // PANEL):
        lo, hi = k * PANEL, (k + 1) * PANEL
        part = jnp.dot(hi_ref[lo:hi, :hi], panel[:hi], preferred_element_type=jnp.float32)
        part += jnp.dot(lo_ref[lo:hi, :hi], panel[:hi], preferred_element_type=jnp.float32)
        parts.append(part.astype(jnp.bfloat16))
    right = jnp.concatenate(parts, axis=0)
    product = jnp.dot(left_ref[...], right, preferred_element_type=jnp.float32)
    value = (cov_ref[...].astype(jnp.float32) - product).astype(jnp.bfloat16)
    keep = jnp.logical_and(row > 0, jnp.logical_or(col > 0, half > 0))
    out_ref[...] = jnp.where(keep, value, jnp.zeros_like(value))


def update(place, cov, rows, mine, other, hi, lo):
    n_rows, n_cols = cov.shape
    vm = pl.BlockSpec(memory_space=pltpu.VMEM)
    tile = pl.BlockSpec((n_rows, TILE), lambda j: (0, j))
    return pl.pallas_call(
        update_kernel,
        out_shape=jax.ShapeDtypeStruct(cov.shape, jnp.bfloat16),
        grid=(n_cols // TILE,),
        in_specs=[pl.BlockSpec(memory_space=pltpu.SMEM), tile, vm, vm, vm, vm, vm],
        out_specs=tile,
        scratch_shapes=[pltpu.VMEM((n_rows, N), jnp.bfloat16)],
        compiler_params=pltpu.CompilerParams(vmem_limit_bytes=24 << 20),
        name="update",
    )(place, cov, rows, mine, other, hi, lo)


CHIPS = 16
PIECE = N // CHIPS
SAME_CORE = [[2 * chip + core for chip in range(CHIPS)] for core in range(2)]


def spread_rows(piece):
    sent = [lax.ppermute(piece, "row", [(0, 8 * x)]) for x in (2, 1, 3)]
    piece = sent[0] + sent[1] + sent[2] + jnp.where(lax.axis_index("row") == 0, piece, 0)
    pairs = lambda y: [(8 * x, 8 * x + 2 * y) for x in range(4)]
    sent = [lax.ppermute(piece, "row", pairs(y)) for y in (3, 2, 1)]
    piece = sent[0] + sent[1] + sent[2] + piece
    return piece + lax.ppermute(piece, "row", [(2 * chip, 2 * chip + 1) for chip in range(CHIPS)])


def scatter(x, axis, groups=None):
    return lax.all_to_all(x, axis, 0, 0, axis_index_groups=groups, tiled=True)[:PIECE]


def gather(piece, axis, groups=None):
    same = jnp.broadcast_to(piece[None], (CHIPS, *piece.shape)).reshape(-1, piece.shape[1])
    return lax.all_to_all(same, axis, 0, 0, axis_index_groups=groups, tiled=True)


def per_device(covariance):
    row = lax.axis_index("row")
    col = lax.axis_index("col")
    core = lax.rem(row, 2)
    first = covariance[:, :N]
    passed = lax.ppermute(covariance[:, N:], "row", [(0, 1)])
    rows_piece = scatter(first, "col")
    cols_piece = scatter(jnp.where(row == 1, passed, first), "row", SAME_CORE)
    leading = gather(spread_rows(rows_piece), "col")
    hi, lo = chol(leading)
    rows = gather(rows_piece, "col")
    mine = gather(cols_piece, "row", SAME_CORE)
    other = lax.ppermute(mine, "row", [(r, r ^ 1) for r in range(2 * CHIPS)])
    place = jnp.stack([row, col, core]).astype(jnp.int32)
    return update(place, covariance, rows, mine, other, hi, lo)


def solution(mesh):
    return jax.shard_map(
        per_device,
        mesh=mesh,
        in_specs=(P("row", "col"),),
        out_specs=P("row", "col"),
        check_vma=False,
    )
```

time: 2450 us -> 241 us (0.10)
  the two profiles are of different devices: /device:TPU:1 before, /device:TPU:50 now
where the time goes in v1:
time: 241 us; the launch traced here: 240 us
  waiting for transfers between devices  79.9 us (33%)
  starting transfers between devices  55 us (23%)
  Pallas kernels  50.4 us (21%)
  blocking collectives  36.6 us (15%)
  local copies, waits for them, and re-layouts  15.1 us (6%)
  other arithmetic  2.92 us (1%)
    pallas_call x1, Pallas kernels, chol(): pl.pallas_call(chol_kernel, out_shape=[jax.ShapeDtypeStruct((N, N), jnp.b...  40 us
    all_to_all x1, blocking collectives, scatter(): lax.all_to_all(x, axis, 0, 0, axis_index_groups=groups, tiled=True)[:PIECE]  36.6 us
    all_to_all x3, waiting for transfers between devices, gather(): lax.all_to_all(same, axis, 0, 0, axis_index_groups=groups, tiled=True)  34.6 us
    all_to_all x1, waiting for transfers between devices, scatter(): lax.all_to_all(x, axis, 0, 0, axis_index_groups=groups, tiled=True)[:PIECE]  32 us
    all_to_all x3, starting transfers between devices, gather(): lax.all_to_all(same, axis, 0, 0, axis_index_groups=groups, tiled=True)  28 us
    all_to_all x1, starting transfers between devices, scatter(): lax.all_to_all(x, axis, 0, 0, axis_index_groups=groups, tiled=True)[:PIECE]  15.7 us
    ppermute x3, waiting for transfers between devices, spread_rows(): sent = [lax.ppermute(piece, 'row', pairs(y)) for y in (3, 2, 1)]  12.3 us
    pallas_call x1, Pallas kernels, update(): pl.pallas_call(update_kernel, out_shape=jax.ShapeDtypeStruct(cov.shape, j...  10.4 us
  transfers between devices with their start and end apart: 13, of which 5 were waited for; matrix products, arithmetic and copies ran while one was open for 3% of the time, Pallas kernels for 17%

profile of v1, /device:TPU:50, one launch (start us, length us, event | category | flops | bytes accessed | tf_op | source)
XLA Modules:
  0.0 240.1 jit_solution(15473728962403583423)
XLA Ops:
  0.0 0.0 copy-start
  0.0 1.5 slice.16
  1.5 1.7 collective-permute-start
  3.2 0.0 collective-permute-done
  3.2 0.0 copy-done
  3.2 1.2 broadcast_select_fusion
  4.4 36.6 %all_to_all.42 = bf16[16,48,768]{2,1,0:T(8,128)(2,1)} all-to-all(bf16[16,48,768]{2,1,0:T(8,128)(2,1)S(1)} %bitcast.16), channel_id=1, replica_groups={{0,32,64,96,128,160,192,224,256,288,320,352,384,416,448,480},{16,48,80,..., dimensions={0} | all-to-all | bytes 2359296 | tf_op jit(solution)/shard_map/all_to_all | solution.py:183
  41.0 15.7 %all-to-all-start = ((bf16[16,48,768]{2,1,0:T(8,128)(2,1)}), bf16[16,48,768]{2,1,0:T(8,128)(2,1)S(1)}, u32[]{:S(2)}, u32[]{:S(2)}) async-start(bf16[16,48,768]{2,1,0:T(8,128)(2,1)} %bitcast.3), calls=%async_computation | async-start | bytes 2359296 | tf_op jit(solution)/shard_map/all_to_all | solution.py:183
  56.7 1.5 slice_bitcast_fusion
  58.2 32.0 %all-to-all-done = bf16[16,48,768]{2,1,0:T(8,128)(2,1)S(1)} async-done(((bf16[16,48,768]{2,1,0:T(8,128)(2,1)}), bf16[16,48,768]{2,1,0:T(8,128)(2,1)S(1)}, u32[]{:S(2)}, u32[]{:S(2)}) %all-to-all-start) | async-done | bytes 1179680 | tf_op jit(solution)/shard_map/all_to_all | solution.py:183
  90.2 0.0 copy-start.5
  90.2 2.0 broadcast_in_dim.29
  92.3 0.0 copy-done.5
  92.3 5.1 %all-to-all-start.3 = ((bf16[16,48,768]{2,1,0:T(8,128)(2,1)}), bf16[16,48,768]{2,1,0:T(8,128)(2,1)S(1)}, u32[]{:S(2)}, u32[]{:S(2)}) async-start(bf16[16,48,768]{2,1,0:T(8,128)(2,1)} %broadcast_in_dim.29), calls=%async_computation.3 | async-start | bytes 2359296 | tf_op jit(solution)/shard_map/all_to_all | solution.py:188
  97.4 1.5 slice_bitcast_fusion.1
  98.9 1.3 collective-permute-start.4
  100.2 1.3 collective-permute-start.3
  101.5 1.3 collective-permute-start.2
  102.8 0.0 collective-permute-done.4
  102.8 0.0 collective-permute-done.3
  102.8 0.0 collective-permute-done.2
  102.8 1.0 select_add_fusion
  103.8 0.7 collective-permute-start.7
  104.5 1.3 collective-permute-start.6
  105.8 0.7 collective-permute-start.5
  106.4 0.0 collective-permute-done.7
  106.4 12.3 %collective-permute-done.6 = bf16[48,768]{1,0:T(8,128)(2,1)S(1)} collective-permute-done((bf16[48,768]{1,0:T(8,128)(2,1)S(1)}, bf16[48,768]{1,0:T(8,128)(2,1)S(1)}, u32[]{:S(2)}, u32[]{:S(2)}) %collective-permute-start.6) | collective-permute-done | bytes 73760 | tf_op jit(solution)/shard_map/ppermute | solution.py:177
  118.8 0.0 collective-permute-done.5
  118.8 1.3 collective-permute-start.8
  120.1 0.9 collective-permute-done.8
  121.0 0.6 add.27
  121.6 2.4 all-to-all-done.3
  124.0 2.0 broadcast_in_dim.31
  126.0 11.6 %all-to-all-start.4 = ((bf16[16,48,768]{2,1,0:T(8,128)(2,1)}), bf16[16,48,768]{2,1,0:T(8,128)(2,1)}, u32[]{:S(2)}, u32[]{:S(2)}) async-start(bf16[16,48,768]{2,1,0:T(8,128)(2,1)} %broadcast_in_dim.31), calls=%async_computation.4 | async-start | bytes 2359296 | tf_op jit(solution)/shard_map/all_to_all | solution.py:188
  137.6 0.1 pad_add_fusion.where_ref
  137.6 1.9 collective-permute-start.1
  139.5 32.3 %all-to-all-done.4 = bf16[16,48,768]{2,1,0:T(8,128)(2,1)} async-done(((bf16[16,48,768]{2,1,0:T(8,128)(2,1)}), bf16[16,48,768]{2,1,0:T(8,128)(2,1)}, u32[]{:S(2)}, u32[]{:S(2)}) %all-to-all-start.4) | async-done | bytes 1179680 | tf_op jit(solution)/shard_map/all_to_all | solution.py:188
  171.8 2.0 broadcast_in_dim.27
  173.8 11.3 %all-to-all-start.1 = ((bf16[16,48,768]{2,1,0:T(8,128)(2,1)}), bf16[16,48,768]{2,1,0:T(8,128)(2,1)}, u32[]{:S(2)}, u32[]{:S(2)}) async-start(bf16[16,48,768]{2,1,0:T(8,128)(2,1)} %broadcast_in_dim.27), calls=%async_computation.1 | async-start | bytes 2359296 | tf_op jit(solution)/shard_map/all_to_all | solution.py:188
  185.0 40.0 %factor.1 = (bf16[768,768]{1,0:T(8,128)(2,1)S(1)}, bf16[768,768]{1,0:T(8,128)(2,1)S(1)}) custom-call(bf16[768,768]{1,0:T(8,128)(2,1)} %bitcast.9.a_ref), custom_call_target="tpu_custom_call" | custom-call | flops 48000000000 | bytes 4000000 | tf_op jit(solution)/shard_map/factor/pallas_call | solution.py:102
  225.0 0.0 copy-start.1
  225.0 1.0 copy-done.1
  226.0 1.0 copy-done.3
  227.1 0.0 all-to-all-done.1
  227.1 0.0 collective-permute-done.1.other_ref
  227.1 1.3 copy-done.2
  228.4 1.3 copy-done.4
  229.6 10.4 %update.1 = bf16[768,1536]{1,0:T(8,128)(2,1)} custom-call(s32[3]{0:T(128)S(1)} %pad_add_fusion.where_ref, bf16[768,1536]{1,0:T(8,128)(2,1)S(1)} %copy-done, bf16[768,768]{1,0:T(8,128)(2,1)} %bitcast.5.rows_ref, bf16[768,768]{1,0:T(8,128)(2,1)S(1)} %bitcast.15, bf16[768,768]{1,0:T(8,128)(2,1)} %collective-permute-done.1.other_ref, ...), custom_call_target="tpu_custom_call" | custom-call | tf_op jit(solution)/shard_map/update/pallas_call | solution.py:156
  (4 shorter events, 0.0 us)
Async XLA Ops:
  0.0 3.2 %copy-start = (bf16[768,1536]{1,0:T(8,128)(2,1)S(1)}, bf16[768,1536]{1,0:T(8,128)(2,1)}, u32[]{:S(2)}) copy-start(bf16[768,1536]{1,0:T(8,128)(2,1)} %cov_ref.1) | copy-start | bytes 7077892
  1.5 1.7 collective-permute-start
  41.0 49.2 %all-to-all-start = ((bf16[16,48,768]{2,1,0:T(8,128)(2,1)}), bf16[16,48,768]{2,1,0:T(8,128)(2,1)S(1)}, u32[]{:S(2)}, u32[]{:S(2)}) async-start(bf16[16,48,768]{2,1,0:T(8,128)(2,1)} %bitcast.3), calls=%async_computation | async-start | bytes 2359296 | tf_op jit(solution)/shard_map/all_to_all | solution.py:183
  90.2 2.0 copy-start.5
  92.3 31.7 %all-to-all-start.3 = ((bf16[16,48,768]{2,1,0:T(8,128)(2,1)}), bf16[16,48,768]{2,1,0:T(8,128)(2,1)S(1)}, u32[]{:S(2)}, u32[]{:S(2)}) async-start(bf16[16,48,768]{2,1,0:T(8,128)(2,1)} %broadcast_in_dim.29), calls=%async_computation.3 | async-start | bytes 2359296 | tf_op jit(solution)/shard_map/all_to_all | solution.py:188
  98.9 3.8 %collective-permute-start.4 = (bf16[48,768]{1,0:T(8,128)(2,1)}, bf16[48,768]{1,0:T(8,128)(2,1)}, u32[]{:S(2)}, u32[]{:S(2)}) collective-permute-start(bf16[48,768]{1,0:T(8,128)(2,1)} %slice_bitcast_fusion.1), channel_id=1, source_target_pairs={{0,384},{1,385},{2,386},{3,387},{4,388},{5,389},{6,390},{7,391},{8... | collective-permute-start | bytes 221192 | tf_op jit(solution)/shard_map/ppermute | solution.py:174
  100.2 2.6 %collective-permute-start.3 = (bf16[48,768]{1,0:T(8,128)(2,1)}, bf16[48,768]{1,0:T(8,128)(2,1)}, u32[]{:S(2)}, u32[]{:S(2)}) collective-permute-start(bf16[48,768]{1,0:T(8,128)(2,1)} %slice_bitcast_fusion.1), channel_id=1, source_target_pairs={{0,128},{1,129},{2,130},{3,131},{4,132},{5,133},{6,134},{7,135},{8... | collective-permute-start | bytes 221192 | tf_op jit(solution)/shard_map/ppermute | solution.py:174
  101.5 1.3 collective-permute-start.2
  103.8 2.6 %collective-permute-start.7 = (bf16[48,768]{1,0:T(8,128)(2,1)S(1)}, bf16[48,768]{1,0:T(8,128)(2,1)S(1)}, u32[]{:S(2)}, u32[]{:S(2)}) collective-permute-start(bf16[48,768]{1,0:T(8,128)(2,1)S(1)} %select_add_fusion), channel_id=1, source_target_pairs={{0,32},{128,160},{256,288},{384,416},{1,33},{129,161},{257,289},{3... | collective-permute-start | bytes 221192 | tf_op jit(solution)/shard_map/ppermute | solution.py:177
  104.5 14.3 %collective-permute-start.6 = (bf16[48,768]{1,0:T(8,128)(2,1)S(1)}, bf16[48,768]{1,0:T(8,128)(2,1)S(1)}, u32[]{:S(2)}, u32[]{:S(2)}) collective-permute-start(bf16[48,768]{1,0:T(8,128)(2,1)S(1)} %select_add_fusion), channel_id=1, source_target_pairs={{0,64},{128,192},{256,320},{384,448},{1,65},{129,193},{257,321},{3... | collective-permute-start | bytes 221192 | tf_op jit(solution)/shard_map/ppermute | solution.py:177
  105.8 13.0 %collective-permute-start.5 = (bf16[48,768]{1,0:T(8,128)(2,1)S(1)}, bf16[48,768]{1,0:T(8,128)(2,1)S(1)}, u32[]{:S(2)}, u32[]{:S(2)}) collective-permute-start(bf16[48,768]{1,0:T(8,128)(2,1)S(1)} %select_add_fusion), channel_id=1, source_target_pairs={{0,96},{128,224},{256,352},{384,480},{1,97},{129,225},{257,353},{3... | collective-permute-start | bytes 221192 | tf_op jit(solution)/shard_map/ppermute | solution.py:177
  118.8 2.2 collective-permute-start.8
  126.0 45.8 %all-to-all-start.4 = ((bf16[16,48,768]{2,1,0:T(8,128)(2,1)}), bf16[16,48,768]{2,1,0:T(8,128)(2,1)}, u32[]{:S(2)}, u32[]{:S(2)}) async-start(bf16[16,48,768]{2,1,0:T(8,128)(2,1)} %broadcast_in_dim.31), calls=%async_computation.4 | async-start | bytes 2359296 | tf_op jit(solution)/shard_map/all_to_all | solution.py:188
  137.6 89.4 %collective-permute-start.1 = (bf16[768,768]{1,0:T(8,128)(2,1)S(1)}, bf16[768,768]{1,0:T(8,128)(2,1)}, u32[]{:S(2)}, u32[]{:S(2)}) collective-permute-start(bf16[768,768]{1,0:T(8,128)(2,1)S(1)} %bitcast.14), channel_id=1, source_target_pairs={{0,16},{16,0},{32,48},{48,32},{64,80},{80,64},{96,112},{112,96},{1... | collective-permute-start | bytes 3538952 | tf_op jit(solution)/shard_map/ppermute | solution.py:203
  173.8 53.3 %all-to-all-start.1 = ((bf16[16,48,768]{2,1,0:T(8,128)(2,1)}), bf16[16,48,768]{2,1,0:T(8,128)(2,1)}, u32[]{:S(2)}, u32[]{:S(2)}) async-start(bf16[16,48,768]{2,1,0:T(8,128)(2,1)} %broadcast_in_dim.27), calls=%async_computation.1 | async-start | bytes 2359296 | tf_op jit(solution)/shard_map/all_to_all | solution.py:188
  225.0 1.0 copy-start.1
  226.0 1.0 copy-start.3
  227.1 1.3 copy-start.2
  228.3 1.3 copy-start.4

commit v2 on v1

--- a/solution.py
+++ b/solution.py
@@ -75,48 +75,93 @@
     return jnp.concatenate(done, axis=0)
 
 
-def chol_kernel(a_ref, hi_ref, lo_ref, s_ref, w_ref):
-    s_ref[...] = a_ref[...].astype(jnp.float32)
+BANDS = STEPS // 2
+FOLD = (STEPS + 1) * B
+SPLIT = 3
+CUT = SPLIT * B
+
+
+def fold(a):
+    bands = []
+    for k in range(BANDS):
+        j = STEPS - 1 - k
+        bands.append(jnp.concatenate([a[k * B : (k + 1) * B, k * B :], a[j * B : (j + 1) * B, j * B :]], axis=1))
+    return jnp.concatenate(bands, axis=0)
+
+
+def eliminate(k, s_ref, w_ref, base):
+    lo, hi = k * B, (k + 1) * B
+    inv = invert_factor(s_ref[lo - base : hi - base, lo - base : hi - base])
+    w_ref[lo:hi, lo:hi] = inv
+    if k:
+        w_ref[lo:hi, :lo] = mm(inv, w_ref[lo:hi, :lo])
+    if hi < N:
+        u = mm(inv, s_ref[lo - base : hi - base, hi - base :])
+        for q in range(k + 1, STEPS):
+            a, b = q * B, (q + 1) * B
+            uq = u[:, a - hi : b - hi]
+            at = slice(a - base, b - base)
+            s_ref[at, a - base :] = s_ref[at, a - base :] - mm_t(uq, u[:, a - hi :])
+            w_ref[a:b, :hi] = w_ref[a:b, :hi] - mm_t(uq, w_ref[lo:hi, :hi])
+
+
+def first_kernel(a_ref, s_out, w_ref, s_ref):
+    for k in range(BANDS):
+        band = a_ref[k * B : (k + 1) * B, :].astype(jnp.float32)
+        j = STEPS - 1 - k
+        s_ref[k * B : (k + 1) * B, k * B :] = band[:, : N - k * B]
+        s_ref[j * B : (j + 1) * B, j * B :] = band[:, N - k * B :]
     w_ref[...] = jnp.zeros_like(w_ref)
-    for k in range(STEPS):
-        lo, hi = k * B, (k + 1) * B
-        inv = invert_factor(s_ref[lo:hi, lo:hi])
-        w_ref[lo:hi, lo:hi] = inv
-        if k:
-            w_ref[lo:hi, :lo] = mm(inv, w_ref[lo:hi, :lo])
-        if hi < N:
-            u = mm(inv, s_ref[lo:hi, hi:])
-            for q in range(k + 1, STEPS):
-                a, b = q * B, (q + 1) * B
-                uq = u[:, a - hi : b - hi]
-                s_ref[a:b, a:] = s_ref[a:b, a:] - mm_t(uq, u[:, a - hi :])
-                w_ref[a:b, :hi] = w_ref[a:b, :hi] - mm_t(uq, w_ref[lo:hi, :hi])
+    for k in range(SPLIT):
+        eliminate(k, s_ref, w_ref, 0)
+    s_out[...] = s_ref[CUT:, CUT:]
+
+
+def second_kernel(s_in, w_in, hi_ref, lo_ref, s_ref, w_ref):
+    s_ref[...] = s_in[...]
+    w_ref[...] = w_in[...]
+    for k in range(SPLIT, STEPS):
+        eliminate(k, s_ref, w_ref, CUT)
     w = w_ref[...]
     high = w.astype(jnp.bfloat16)
     hi_ref[...] = high
     lo_ref[...] = (w - high.astype(jnp.float32)).astype(jnp.bfloat16)
 
 
-def chol(a):
+def factor(folded):
     vm = pl.BlockSpec(memory_space=pltpu.VMEM)
-    return pl.pallas_call(
-        chol_kernel,
-        out_shape=[jax.ShapeDtypeStruct((N, N), jnp.bfloat16)] * 2,
+    f32 = jnp.float32
+    cost = pl.CostEstimate(flops=20_000_000_000, bytes_accessed=4_000_000, transcendentals=0)
+    params = pltpu.CompilerParams(vmem_limit_bytes=16 << 20)
+    rest = N - CUT
+    state = pl.pallas_call(
+        first_kernel,
+        out_shape=[jax.ShapeDtypeStruct((rest, rest), f32), jax.ShapeDtypeStruct((N, N), f32)],
         in_specs=[vm],
         out_specs=[vm, vm],
-        scratch_shapes=[pltpu.VMEM((N, N), jnp.float32), pltpu.VMEM((N, N), jnp.float32)],
-        compiler_params=pltpu.CompilerParams(vmem_limit_bytes=16 << 20),
-        cost_estimate=pl.CostEstimate(flops=48_000_000_000, bytes_accessed=4_000_000, transcendentals=0),
-        name="factor",
-    )(a)
+        scratch_shapes=[pltpu.VMEM((N, N), f32)],
+        compiler_params=params,
+        cost_estimate=cost,
+        name="factor_first",
+    )(folded)
+    return state, lambda s, w: pl.pallas_call(
+        second_kernel,
+        out_shape=[jax.ShapeDtypeStruct((N, N), jnp.bfloat16)] * 2,
+        in_specs=[vm, vm],
+        out_specs=[vm, vm],
+        scratch_shapes=[pltpu.VMEM((rest, rest), f32), pltpu.VMEM((N, N), f32)],
+        compiler_params=params,
+        cost_estimate=cost,
+        name="factor_second",
+    )(s, w)
 
 
 TILE = 256
 PANEL = 256
 
 
-def update_kernel(where_ref, cov_ref, rows_ref, mine_ref, other_ref, hi_ref, lo_ref, out_ref, left_ref):
-    row, col, core = where_ref[0], where_ref[1], where_ref[2]
+def update_kernel(where_ref, cov_ref, rows_ref, cols_ref, hi_ref, lo_ref, out_ref, left_ref):
+    row, col = where_ref[0], where_ref[1]
     step = pl.program_id(0)
 
     @pl.when(step == 0)
@@ -134,8 +179,7 @@
             left_ref[:, lo:hi] = part.astype(jnp.bfloat16)
 
     half = lax.div(step, N // TILE)
-    at = pl.multiple_of(lax.rem(step, N // TILE) * TILE, TILE)
-    panel = jnp.where(half == core, mine_ref[:, pl.ds(at, TILE)], other_ref[:, pl.ds(at, TILE)])
+    panel = cols_ref[...]
     parts = []
     for k in range(N // PANEL):
         lo, hi = k * PANEL, (k + 1) * PANEL
@@ -149,7 +193,7 @@
     out_ref[...] = jnp.where(keep, value, jnp.zeros_like(value))
 
 
-def update(place, cov, rows, mine, other, hi, lo):
+def update(place, cov, rows, cols, hi, lo):
     n_rows, n_cols = cov.shape
     vm = pl.BlockSpec(memory_space=pltpu.VMEM)
     tile = pl.BlockSpec((n_rows, TILE), lambda j: (0, j))
@@ -157,52 +201,84 @@
         update_kernel,
         out_shape=jax.ShapeDtypeStruct(cov.shape, jnp.bfloat16),
         grid=(n_cols // TILE,),
-        in_specs=[pl.BlockSpec(memory_space=pltpu.SMEM), tile, vm, vm, vm, vm, vm],
+        in_specs=[pl.BlockSpec(memory_space=pltpu.SMEM), tile, vm, pl.BlockSpec((N, TILE), lambda j: (0, j)), vm, vm],
         out_specs=tile,
         scratch_shapes=[pltpu.VMEM((n_rows, N), jnp.bfloat16)],
         compiler_params=pltpu.CompilerParams(vmem_limit_bytes=24 << 20),
         name="update",
-    )(place, cov, rows, mine, other, hi, lo)
-
-
-CHIPS = 16
-PIECE = N // CHIPS
-SAME_CORE = [[2 * chip + core for chip in range(CHIPS)] for core in range(2)]
-
-
-def spread_rows(piece):
-    sent = [lax.ppermute(piece, "row", [(0, 8 * x)]) for x in (2, 1, 3)]
-    piece = sent[0] + sent[1] + sent[2] + jnp.where(lax.axis_index("row") == 0, piece, 0)
-    pairs = lambda y: [(8 * x, 8 * x + 2 * y) for x in range(4)]
-    sent = [lax.ppermute(piece, "row", pairs(y)) for y in (3, 2, 1)]
-    piece = sent[0] + sent[1] + sent[2] + piece
-    return piece + lax.ppermute(piece, "row", [(2 * chip, 2 * chip + 1) for chip in range(CHIPS)])
-
-
-def scatter(x, axis, groups=None):
-    return lax.all_to_all(x, axis, 0, 0, axis_index_groups=groups, tiled=True)[:PIECE]
-
-
-def gather(piece, axis, groups=None):
-    same = jnp.broadcast_to(piece[None], (CHIPS, *piece.shape)).reshape(-1, piece.shape[1])
-    return lax.all_to_all(same, axis, 0, 0, axis_index_groups=groups, tiled=True)
+    )(place, cov, rows, cols, hi, lo)
+
+
+DEPTH = 8
+PART = N // 4
+AXES = ("row", "col")
+
+
+def device(x, y, z, core):
+    return ((x % 4 * 4 + y % 4) * 2 + core) * 2 * DEPTH + (y % 8 // 4) * DEPTH + z % DEPTH
+
+
+def send(x, pairs):
+    return lax.ppermute(x, AXES, pairs)
+
+
+def chips(xs, ys, zs):
+    return [(x, y, z) for x in xs for y in ys for z in zs]
+
+
+def shifts(sources, by, cores=(0,)):
+    return [
+        (device(x, y, z, c), device(x + by[0], y + by[1], z + by[2], c)) for x, y, z in sources for c in cores
+    ]
+
+
+def fan(x, sources, offsets, cores=(0,)):
+    return sum([send(x, shifts(sources, by, cores)) for by in offsets], x)
+
+
+def scatter(x, size, sources, offsets, cores=(0,)):
+    sent = [
+        send(x[i * size : (i + 1) * size], shifts(sources, by, cores)) for i, by in enumerate(offsets, 1)
+    ]
+    return sum(sent, x[:size])
 
 
 def per_device(covariance):
     row = lax.axis_index("row")
     col = lax.axis_index("col")
-    core = lax.rem(row, 2)
-    first = covariance[:, :N]
-    passed = lax.ppermute(covariance[:, N:], "row", [(0, 1)])
-    rows_piece = scatter(first, "col")
-    cols_piece = scatter(jnp.where(row == 1, passed, first), "row", SAME_CORE)
-    leading = gather(spread_rows(rows_piece), "col")
-    hi, lo = chol(leading)
-    rows = gather(rows_piece, "col")
-    mine = gather(cols_piece, "row", SAME_CORE)
-    other = lax.ppermute(mine, "row", [(r, r ^ 1) for r in range(2 * CHIPS)])
-    place = jnp.stack([row, col, core]).astype(jnp.int32)
-    return update(place, covariance, rows, mine, other, hi, lo)
+    place = jnp.stack([row, col]).astype(jnp.int32)
+
+    leading = jnp.where(jnp.logical_and(row == 0, col == 0), fold(covariance[:, :N]), 0)
+    along_x = [(1, 0, 0), (2, 0, 0), (3, 0, 0)]
+    leading = scatter(leading, leading.shape[0] // 4, [(0, 0, 0)], along_x)
+    leading = fan(leading, chips(range(4), [0], [0]), [(0, 0, 4), (0, 0, 2), (0, 0, 6)])
+    leading = fan(leading, chips(range(4), [0], range(0, 8, 2)), [(0, 4, 1), (0, 4, 0), (0, 0, 1)])
+    leading = fan(leading, chips(range(4), [0, 4], range(8)), [(0, 2, 0), (0, 1, 0), (0, 7, 0)])
+    leading = leading + lax.ppermute(leading, "row", [(2 * chip, 2 * chip + 1) for chip in range(16)])
+    same_x = [[8 * x + i for x in range(4)] for i in range(8)]
+    leading = lax.all_gather(leading, "row", axis=0, tiled=True, axis_index_groups=same_x)
+
+    columns = chips([0], [0, 4], range(8))
+    cols = jnp.where(row == 0, covariance, 0)
+    cols = scatter(cols, PART, columns, along_x)
+    cols = scatter(cols, PART // 4, chips(range(4), [0, 4], range(8)), [(0, 1, 0), (0, 2, 0), (0, 3, 0)])
+    half = cols.shape[0] // 2
+    other = lax.ppermute(cols[half:], "row", [(2 * chip, 2 * chip + 1) for chip in range(16)])
+    cols = jnp.where(row % 2 == 0, cols[:half], other)
+    cols = lax.all_gather(cols, "row", axis=0, tiled=True)
+
+    both = (0, 1)
+    rows = jnp.where(col == 0, covariance[:, :N], 0)
+    rows = scatter(rows, PART, chips(range(4), range(4), [0]), [(0, 0, 2), (0, 0, 4), (0, 0, 6)], both)
+    rows = fan(rows, chips(range(4), range(4), range(0, 8, 2)), [(0, 0, 1)], both)
+    rows = fan(rows, chips(range(4), range(4), range(8)), [(0, 4, 0)], both)
+    same_z = [[8 * y + odd + 2 * z for z in range(4)] for y in range(2) for odd in range(2)]
+    copies = jnp.broadcast_to(rows[None], (4, *rows.shape)).reshape(N, N)
+
+    (s, w), finish = factor(leading)
+    rows = lax.all_to_all(copies, "col", 0, 0, axis_index_groups=same_z, tiled=True)
+    hi, lo = finish(s, w)
+    return update(place, covariance, rows, cols, hi, lo)
 
 
 def solution(mesh):

time: 241 us -> 177 us (0.73)
  the two profiles are of different devices: /device:TPU:50 before, /device:TPU:24 now
where the time goes in v2:
time: 177 us; the launch traced here: 176 us
  starting transfers between devices  54.3 us (31%)
  Pallas kernels  48.4 us (27%)
  local copies, waits for them, and re-layouts  21.6 us (12%)
  waiting for transfers between devices  16.4 us (9%)
  blocking collectives  14.5 us (8%)
  between operations  13.8 us (8%)
  other arithmetic  7.24 us (4%)
    ppermute x23, starting transfers between devices, send(): return lax.ppermute(x, AXES, pairs)  48.1 us
    pallas_call x1, Pallas kernels, factor(): pl.pallas_call(first_kernel, out_shape=[jax.ShapeDtypeStruct((rest, rest)...  20.3 us
    pallas_call x1, Pallas kernels, factor(): pl.pallas_call(second_kernel, out_shape=[jax.ShapeDtypeStruct((N, N), jnp...  18.8 us
    ppermute x23, waiting for transfers between devices, send(): return lax.ppermute(x, AXES, pairs)  16.4 us
    all_gather x1, blocking collectives, per_device(): lax.all_gather(leading, 'row', axis=0, tiled=True, axis_index_groups=same_x)  14.5 us
    unnamed x24, local copies, waits for them, and re-layouts  11.8 us
    pallas_call x1, Pallas kernels, update(): pl.pallas_call(update_kernel, out_shape=jax.ShapeDtypeStruct(cov.shape, j...  9.33 us
    add x4, other arithmetic, scatter(): return sum(sent, x[:size])  4.07 us
  transfers between devices with their start and end apart: 27, of which 2 were waited for; matrix products, arithmetic and copies ran while one was open for 6% of the time, Pallas kernels for 22%

profile of v2, /device:TPU:24, one launch (start us, length us, event | category | flops | bytes accessed | tf_op | source)
XLA Modules:
  0.0 176.2 jit_solution(16354644518363896249)
XLA Ops:
  6.5 0.9 slice.97
  7.5 0.9 slice.99
  8.4 0.9 slice.101
  9.3 1.1 slice.102
  10.4 0.8 slice.100
  11.3 0.8 slice.98
  12.1 0.9 fusion.10
  13.0 1.3 collective-permute-start.12
  14.3 1.3 collective-permute-start.13
  15.8 1.3 fusion.8
  17.8 1.5 collective-permute-start.5
  19.3 1.5 collective-permute-start.6
  20.7 1.5 collective-permute-start.7
  22.3 0.7 collective-permute-start.14
  23.0 1.0 fusion.9
  24.0 6.8 %collective-permute-start = (bf16[192,768]{1,0:T(8,128)(2,1)}, bf16[192,768]{1,0:T(8,128)(2,1)}, u32[]{:S(2)}, u32[]{:S(2)}) collective-permute-start(bf16[192,768]{1,0:T(8,128)(2,1)} %get-tuple-element.16), channel_id=1, source_target_pairs={{0,2},{16,18},{32,34},{48,50},{64,66},{80,82},{96,98},{112,114},{1... | collective-permute-start | bytes 884744 | tf_op jit(solution)/shard_map/ppermute | solution.py:222
  30.8 6.2 %collective-permute-start.1 = (bf16[192,768]{1,0:T(8,128)(2,1)}, bf16[192,768]{1,0:T(8,128)(2,1)}, u32[]{:S(2)}, u32[]{:S(2)}) collective-permute-start(bf16[192,768]{1,0:T(8,128)(2,1)} %get-tuple-element.18), channel_id=1, source_target_pairs={{0,4},{16,20},{32,36},{48,52},{64,68},{80,84},{96,100},{112,116},{... | collective-permute-start | bytes 884744 | tf_op jit(solution)/shard_map/ppermute | solution.py:222
  37.0 1.1 fusion.5
  40.2 1.7 fusion.1
  41.9 1.3 collective-permute-start.10
  44.7 8.7 %collective-permute-done.10 = bf16[48,1536]{1,0:T(8,128)(2,1)S(1)} collective-permute-done((bf16[48,1536]{1,0:T(8,128)(2,1)S(1)}, bf16[48,1536]{1,0:T(8,128)(2,1)S(1)}, u32[]{:S(2)}, u32[]{:S(2)}) %collective-permute-start.10) | collective-permute-done | bytes 147488 | tf_op jit(solution)/shard_map/ppermute | solution.py:222
  55.4 2.0 %collective-permute-start.2 = (bf16[192,768]{1,0:T(8,128)(2,1)}, bf16[192,768]{1,0:T(8,128)(2,1)}, u32[]{:S(2)}, u32[]{:S(2)}) collective-permute-start(bf16[192,768]{1,0:T(8,128)(2,1)} %get-tuple-element.17), channel_id=1, source_target_pairs={{0,6},{16,22},{32,38},{48,54},{64,70},{80,86},{96,102},{112,118},{... | collective-permute-start | bytes 884744 | tf_op jit(solution)/shard_map/ppermute | solution.py:222
  57.5 1.3 collective-permute-start.11
  58.8 0.7 add_add_fusion.1
  59.5 1.3 collective-permute-start.21
  60.8 1.3 collective-permute-start.22
  62.8 1.3 collective-permute-start.23
  64.1 1.2 fusion.3
  65.3 1.3 collective-permute-start.3
  66.7 7.7 %collective-permute-done.23 = bf16[96,896]{1,0:T(8,128)(2,1)S(1)} collective-permute-done((bf16[96,896]{1,0:T(8,128)(2,1)}, bf16[96,896]{1,0:T(8,128)(2,1)S(1)}, u32[]{:S(2)}, u32[]{:S(2)}) %collective-permute-start.23) | collective-permute-done | bytes 172064 | tf_op jit(solution)/shard_map/ppermute | solution.py:222
  74.3 1.1 add_add_fusion
  75.5 1.3 collective-permute-start.24
  76.9 13.5 %collective-permute-start.4 = (bf16[192,768]{1,0:T(8,128)(2,1)S(1)}, bf16[192,768]{1,0:T(8,128)(2,1)S(1)}, u32[]{:S(2)}, u32[]{:S(2)}) collective-permute-start(bf16[192,768]{1,0:T(8,128)(2,1)S(1)} %add.79), channel_id=1, source_target_pairs={{0,8},{16,24},{1,9},{17,25},{2,10},{18,26},{3,11},{19,27},{4,12},{... | collective-permute-start | bytes 884744 | tf_op jit(solution)/shard_map/ppermute | solution.py:222
  90.5 14.5 %all_gather.7.a_ref = bf16[384,896]{1,0:T(8,128)(2,1)S(1)} all-gather(bf16[96,896]{1,0:T(8,128)(2,1)S(1)} %add.100), channel_id=1, replica_groups={{0,128,256,384},{16,144,272,400},{32,160,288,416},{48,176,304,432},{64,..., dimensions={0}, use_global_device_ids=true | all-gather | bytes 860160 | tf_op jit(solution)/shard_map/all_gather | solution.py:259
  105.0 20.3 %factor_first.1 = (f32[384,384]{1,0:T(8,128)S(1)}, f32[768,768]{1,0:T(8,128)S(1)}) custom-call(bf16[384,896]{1,0:T(8,128)(2,1)S(1)} %all_gather.7.a_ref), custom_call_target="tpu_custom_call" | custom-call | flops 20000000000 | bytes 4000000 | tf_op jit(solution)/shard_map/factor_first/pallas_call | solution.py:137
  125.3 1.4 copy-done.6
  126.7 0.8 copy-done.8
  127.6 1.1 broadcast_in_dim.19
  128.7 3.5 %all-to-all-start = ((bf16[4,192,768]{2,1,0:T(8,128)(2,1)}), bf16[4,192,768]{2,1,0:T(8,128)(2,1)S(1)}, u32[]{:S(2)}, u32[]{:S(2)}) async-start(bf16[4,192,768]{2,1,0:T(8,128)(2,1)} %broadcast_in_dim.19), calls=%async_computation | async-start | bytes 2359296 | tf_op jit(solution)/shard_map/all_to_all | solution.py:279
  132.3 1.7 copy-done.7
  133.9 1.1 copy-done.9
  135.0 18.8 %factor_second.1 = (bf16[768,768]{1,0:T(8,128)(2,1)S(1)}, bf16[768,768]{1,0:T(8,128)(2,1)S(1)}) custom-call(f32[384,384]{1,0:T(8,128)S(1)} %copy-done.9, f32[768,768]{1,0:T(8,128)S(1)} %copy-done.7), custom_call_target="tpu_custom_call" | custom-call | flops 20000000000 | bytes 4000000 | tf_op jit(solution)/shard_map/factor_second/pallas_call | solution.py:147
  153.8 1.0 copy-done.2
  154.8 1.0 copy-done.4
  155.8 1.7 copy-done.1
  157.5 1.3 copy-done.3
  158.7 1.3 copy-done.5
  160.0 9.3 %update.1 = bf16[768,1536]{1,0:T(8,128)(2,1)} custom-call(s32[2]{0:T(128)S(1)} %pad_add_fusion.where_ref, bf16[768,1536]{1,0:T(8,128)(2,1)S(1)} %copy-done, bf16[768,768]{1,0:T(8,128)(2,1)S(1)} %bitcast.3, bf16[768,1536]{1,0:T(8,128)(2,1)S(1)} %copy-done.1, bf16[768,768]{1,0:T(8,128)(2,1)S(1)} %copy-done.3, bf16[768,768]{1,0:T(8,128)(2,1)S(1)} %copy-done.5), custom_call_target="tpu_custom_call" | custom-call | tf_op jit(solution)/shard_map/update/pallas_call | solution.py:200
  (62 shorter events, 7.5 us)
Async XLA Ops:
  6.5 149.3 %all-gather.2.cloned.1.call-start = ((), (), s32[]{:S(2)}) async-start(), calls=%async_computation.1 | async-start | bytes 2433024 | tf_op jit(solution)/shard_map/all_gather | solution.py:268
  9.3 6.3 %copy-start = (bf16[768,1536]{1,0:T(8,128)(2,1)S(1)}, bf16[768,1536]{1,0:T(8,128)(2,1)}, u32[]{:S(2)}) copy-start(bf16[768,1536]{1,0:T(8,128)(2,1)} %cov_ref.1) | copy-start | bytes 7077892
  12.1 2.2 %copy-start.11 = (bf16[384,896]{1,0:T(8,128)(2,1)}, bf16[384,896]{1,0:T(8,128)(2,1)S(1)}, u32[]{:S(2)}) copy-start(bf16[384,896]{1,0:T(8,128)(2,1)S(1)} %maximum_select_fusion) | copy-start | bytes 2064388
  13.0 9.3 %collective-permute-start.12 = (bf16[96,896]{1,0:T(8,128)(2,1)}, bf16[96,896]{1,0:T(8,128)(2,1)}, u32[]{:S(2)}, u32[]{:S(2)}) collective-permute-start(bf16[96,896]{1,0:T(8,128)(2,1)} %get-tuple-element.19), channel_id=1, source_target_pairs={{0,128}} | collective-permute-start | bytes 516104 | tf_op jit(solution)/shard_map/ppermute | solution.py:222
  14.3 9.6 %collective-permute-start.13 = (bf16[96,896]{1,0:T(8,128)(2,1)}, bf16[96,896]{1,0:T(8,128)(2,1)}, u32[]{:S(2)}, u32[]{:S(2)}) collective-permute-start(bf16[96,896]{1,0:T(8,128)(2,1)} %get-tuple-element.21), channel_id=1, source_target_pairs={{0,256}} | collective-permute-start | bytes 516104 | tf_op jit(solution)/shard_map/ppermute | solution.py:222
  15.8 2.0 %copy-start.10 = (bf16[768,1536]{1,0:T(8,128)(2,1)}, bf16[768,1536]{1,0:T(8,128)(2,1)S(1)}, u32[]{:S(2)}) copy-start(bf16[768,1536]{1,0:T(8,128)(2,1)S(1)} %broadcast_select_fusion) | copy-start | bytes 7077892
  17.8 20.3 %collective-permute-start.5 = (bf16[192,1536]{1,0:T(8,128)(2,1)}, bf16[192,1536]{1,0:T(8,128)(2,1)}, u32[]{:S(2)}, u32[]{:S(2)}) collective-permute-start(bf16[192,1536]{1,0:T(8,128)(2,1)} %get-tuple-element.13), channel_id=1, source_target_pairs={{0,128},{1,129},{2,130},{3,131},{4,132},{5,133},{6,134},{7,135},{8... | collective-permute-start | bytes 1769480 | tf_op jit(solution)/shard_map/ppermute | solution.py:222
  19.3 19.5 %collective-permute-start.6 = (bf16[192,1536]{1,0:T(8,128)(2,1)}, bf16[192,1536]{1,0:T(8,128)(2,1)}, u32[]{:S(2)}, u32[]{:S(2)}) collective-permute-start(bf16[192,1536]{1,0:T(8,128)(2,1)} %get-tuple-element.15), channel_id=1, source_target_pairs={{0,256},{1,257},{2,258},{3,259},{4,260},{5,261},{6,262},{7,263},{8... | collective-permute-start | bytes 1769480 | tf_op jit(solution)/shard_map/ppermute | solution.py:222
  20.7 18.7 %collective-permute-start.7 = (bf16[192,1536]{1,0:T(8,128)(2,1)}, bf16[192,1536]{1,0:T(8,128)(2,1)}, u32[]{:S(2)}, u32[]{:S(2)}) collective-permute-start(bf16[192,1536]{1,0:T(8,128)(2,1)} %get-tuple-element.14), channel_id=1, source_target_pairs={{0,384},{1,385},{2,386},{3,387},{4,388},{5,389},{6,390},{7,391},{8... | collective-permute-start | bytes 1769480 | tf_op jit(solution)/shard_map/ppermute | solution.py:222
  22.3 8.4 %collective-permute-start.14 = (bf16[96,896]{1,0:T(8,128)(2,1)}, bf16[96,896]{1,0:T(8,128)(2,1)S(1)}, u32[]{:S(2)}, u32[]{:S(2)}) collective-permute-start(bf16[96,896]{1,0:T(8,128)(2,1)} %get-tuple-element.20), channel_id=1, source_target_pairs={{0,384}} | collective-permute-start | bytes 516104 | tf_op jit(solution)/shard_map/ppermute | solution.py:222
  24.0 38.8 %collective-permute-start = (bf16[192,768]{1,0:T(8,128)(2,1)}, bf16[192,768]{1,0:T(8,128)(2,1)}, u32[]{:S(2)}, u32[]{:S(2)}) collective-permute-start(bf16[192,768]{1,0:T(8,128)(2,1)} %get-tuple-element.16), channel_id=1, source_target_pairs={{0,2},{16,18},{32,34},{48,50},{64,66},{80,82},{96,98},{112,114},{1... | collective-permute-start | bytes 884744 | tf_op jit(solution)/shard_map/ppermute | solution.py:222
  30.8 33.3 %collective-permute-start.1 = (bf16[192,768]{1,0:T(8,128)(2,1)}, bf16[192,768]{1,0:T(8,128)(2,1)}, u32[]{:S(2)}, u32[]{:S(2)}) collective-permute-start(bf16[192,768]{1,0:T(8,128)(2,1)} %get-tuple-element.18), channel_id=1, source_target_pairs={{0,4},{16,20},{32,36},{48,52},{64,68},{80,84},{96,100},{112,116},{... | collective-permute-start | bytes 884744 | tf_op jit(solution)/shard_map/ppermute | solution.py:222
  38.1 3.8 %collective-permute-start.15 = (bf16[96,896]{1,0:T(8,128)(2,1)S(1)}, bf16[96,896]{1,0:T(8,128)(2,1)S(1)}, u32[]{:S(2)}, u32[]{:S(2)}) collective-permute-start(bf16[96,896]{1,0:T(8,128)(2,1)S(1)} %fusion.5), channel_id=1, source_target_pairs={{0,4},{128,132},{256,260},{384,388}} | collective-permute-start | bytes 516104 | tf_op jit(solution)/shard_map/ppermute | solution.py:222
  38.8 4.4 %collective-permute-start.16 = (bf16[96,896]{1,0:T(8,128)(2,1)S(1)}, bf16[96,896]{1,0:T(8,128)(2,1)S(1)}, u32[]{:S(2)}, u32[]{:S(2)}) collective-permute-start(bf16[96,896]{1,0:T(8,128)(2,1)S(1)} %fusion.5), channel_id=1, source_target_pairs={{0,2},{128,130},{256,258},{384,386}} | collective-permute-start | bytes 516104 | tf_op jit(solution)/shard_map/ppermute | solution.py:222
  39.5 4.4 %collective-permute-start.17 = (bf16[96,896]{1,0:T(8,128)(2,1)S(1)}, bf16[96,896]{1,0:T(8,128)(2,1)S(1)}, u32[]{:S(2)}, u32[]{:S(2)}) collective-permute-start(bf16[96,896]{1,0:T(8,128)(2,1)S(1)} %fusion.5), channel_id=1, source_target_pairs={{0,6},{128,134},{256,262},{384,390}} | collective-permute-start | bytes 516104 | tf_op jit(solution)/shard_map/ppermute | solution.py:222
  41.9 11.4 %collective-permute-start.10 = (bf16[48,1536]{1,0:T(8,128)(2,1)S(1)}, bf16[48,1536]{1,0:T(8,128)(2,1)S(1)}, u32[]{:S(2)}, u32[]{:S(2)}) collective-permute-start(bf16[48,1536]{1,0:T(8,128)(2,1)S(1)} %get-tuple-element.23), channel_id=1, source_target_pairs={{0,96},{1,97},{2,98},{3,99},{4,100},{5,101},{6,102},{7,103},{8,104... | collective-permute-start | bytes 442376 | tf_op jit(solution)/shard_map/ppermute | solution.py:222
  43.2 10.8 %collective-permute-start.8 = (bf16[48,1536]{1,0:T(8,128)(2,1)S(1)}, bf16[48,1536]{1,0:T(8,128)(2,1)S(1)}, u32[]{:S(2)}, u32[]{:S(2)}) collective-permute-start(bf16[48,1536]{1,0:T(8,128)(2,1)S(1)} %get-tuple-element.22), channel_id=1, source_target_pairs={{0,32},{1,33},{2,34},{3,35},{4,36},{5,37},{6,38},{7,39},{8,40},{9,... | collective-permute-start | bytes 442376 | tf_op jit(solution)/shard_map/ppermute | solution.py:222
  43.9 10.8 %collective-permute-start.9 = (bf16[48,1536]{1,0:T(8,128)(2,1)S(1)}, bf16[48,1536]{1,0:T(8,128)(2,1)S(1)}, u32[]{:S(2)}, u32[]{:S(2)}) collective-permute-start(bf16[48,1536]{1,0:T(8,128)(2,1)S(1)} %get-tuple-element.24), channel_id=1, source_target_pairs={{0,64},{1,65},{2,66},{3,67},{4,68},{5,69},{6,70},{7,71},{8,72},{9,... | collective-permute-start | bytes 442376 | tf_op jit(solution)/shard_map/ppermute | solution.py:222
  53.3 2.1 %collective-permute-start.18 = (bf16[96,896]{1,0:T(8,128)(2,1)S(1)}, bf16[96,896]{1,0:T(8,128)(2,1)S(1)}, u32[]{:S(2)}, u32[]{:S(2)}) collective-permute-start(bf16[96,896]{1,0:T(8,128)(2,1)S(1)} %add_add_fusion.2), channel_id=1, source_target_pairs={{0,9},{2,11},{4,13},{6,15},{128,137},{130,139},{132,141},{134,143}... | collective-permute-start | bytes 516104 | tf_op jit(solution)/shard_map/ppermute | solution.py:222
  54.0 3.5 %collective-permute-start.19 = (bf16[96,896]{1,0:T(8,128)(2,1)S(1)}, bf16[96,896]{1,0:T(8,128)(2,1)S(1)}, u32[]{:S(2)}, u32[]{:S(2)}) collective-permute-start(bf16[96,896]{1,0:T(8,128)(2,1)S(1)} %add_add_fusion.2), channel_id=1, source_target_pairs={{0,8},{2,10},{4,12},{6,14},{128,136},{130,138},{132,140},{134,142}... | collective-permute-start | bytes 516104 | tf_op jit(solution)/shard_map/ppermute | solution.py:222
  54.7 4.1 %collective-permute-start.20 = (bf16[96,896]{1,0:T(8,128)(2,1)S(1)}, bf16[96,896]{1,0:T(8,128)(2,1)S(1)}, u32[]{:S(2)}, u32[]{:S(2)}) collective-permute-start(bf16[96,896]{1,0:T(8,128)(2,1)S(1)} %add_add_fusion.2), channel_id=1, source_target_pairs={{0,1},{2,3},{4,5},{6,7},{128,129},{130,131},{132,133},{134,135},{2... | collective-permute-start | bytes 516104 | tf_op jit(solution)/shard_map/ppermute | solution.py:222
  55.4 8.7 %collective-permute-start.2 = (bf16[192,768]{1,0:T(8,128)(2,1)}, bf16[192,768]{1,0:T(8,128)(2,1)}, u32[]{:S(2)}, u32[]{:S(2)}) collective-permute-start(bf16[192,768]{1,0:T(8,128)(2,1)} %get-tuple-element.17), channel_id=1, source_target_pairs={{0,6},{16,22},{32,38},{48,54},{64,70},{80,86},{96,102},{112,118},{... | collective-permute-start | bytes 884744 | tf_op jit(solution)/shard_map/ppermute | solution.py:222
  57.5 3.3 %collective-permute-start.11 = (bf16[24,1536]{1,0:T(8,128)(2,1)S(1)}, bf16[24,1536]{1,0:T(8,128)(2,1)S(1)}, u32[]{:S(2)}, u32[]{:S(2)}) collective-permute-start(bf16[24,1536]{1,0:T(8,128)(2,1)S(1)} %slice.120), channel_id=1, source_target_pairs={{0,16},{32,48},{64,80},{96,112},{128,144},{160,176},{192,208},{224... | collective-permute-start | bytes 221192 | tf_op jit(solution)/shard_map/ppermute | solution.py:266
  59.5 7.2 %collective-permute-start.21 = (bf16[96,896]{1,0:T(8,128)(2,1)}, bf16[96,896]{1,0:T(8,128)(2,1)}, u32[]{:S(2)}, u32[]{:S(2)}) collective-permute-start(bf16[96,896]{1,0:T(8,128)(2,1)} %add_add_fusion.1), channel_id=1, source_target_pairs={{0,64},{1,65},{2,66},{3,67},{4,68},{5,69},{6,70},{7,71},{8,72},{9,... | collective-permute-start | bytes 516104 | tf_op jit(solution)/shard_map/ppermute | solution.py:222
  60.8 5.9 %collective-permute-start.22 = (bf16[96,896]{1,0:T(8,128)(2,1)}, bf16[96,896]{1,0:T(8,128)(2,1)}, u32[]{:S(2)}, u32[]{:S(2)}) collective-permute-start(bf16[96,896]{1,0:T(8,128)(2,1)} %add_add_fusion.1), channel_id=1, source_target_pairs={{0,32},{1,33},{2,34},{3,35},{4,36},{5,37},{6,38},{7,39},{8,40},{9,... | collective-permute-start | bytes 516104 | tf_op jit(solution)/shard_map/ppermute | solution.py:222
  62.8 11.5 %collective-permute-start.23 = (bf16[96,896]{1,0:T(8,128)(2,1)}, bf16[96,896]{1,0:T(8,128)(2,1)S(1)}, u32[]{:S(2)}, u32[]{:S(2)}) collective-permute-start(bf16[96,896]{1,0:T(8,128)(2,1)} %add_add_fusion.1), channel_id=1, source_target_pairs={{0,104},{1,105},{2,106},{3,107},{4,108},{5,109},{6,110},{7,111},{8... | collective-permute-start | bytes 516104 | tf_op jit(solution)/shard_map/ppermute | solution.py:222
  65.3 11.5 %collective-permute-start.3 = (bf16[192,768]{1,0:T(8,128)(2,1)S(1)}, bf16[192,768]{1,0:T(8,128)(2,1)S(1)}, u32[]{:S(2)}, u32[]{:S(2)}) collective-permute-start(bf16[192,768]{1,0:T(8,128)(2,1)S(1)} %fusion.3), channel_id=1, source_target_pairs={{0,1},{16,17},{2,3},{18,19},{4,5},{20,21},{6,7},{22,23},{32,33},{4... | collective-permute-start | bytes 884744 | tf_op jit(solution)/shard_map/ppermute | solution.py:222
  75.5 15.0 %collective-permute-start.24 = (bf16[96,896]{1,0:T(8,128)(2,1)S(1)}, bf16[96,896]{1,0:T(8,128)(2,1)S(1)}, u32[]{:S(2)}, u32[]{:S(2)}) collective-permute-start(bf16[96,896]{1,0:T(8,128)(2,1)S(1)} %add_add_fusion), channel_id=1, source_target_pairs={{0,16},{32,48},{64,80},{96,112},{128,144},{160,176},{192,208},{224... | collective-permute-start | bytes 516104 | tf_op jit(solution)/shard_map/ppermute | solution.py:257
  76.9 50.6 %collective-permute-start.4 = (bf16[192,768]{1,0:T(8,128)(2,1)S(1)}, bf16[192,768]{1,0:T(8,128)(2,1)S(1)}, u32[]{:S(2)}, u32[]{:S(2)}) collective-permute-start(bf16[192,768]{1,0:T(8,128)(2,1)S(1)} %add.79), channel_id=1, source_target_pairs={{0,8},{16,24},{1,9},{17,25},{2,10},{18,26},{3,11},{19,27},{4,12},{... | collective-permute-start | bytes 884744 | tf_op jit(solution)/shard_map/ppermute | solution.py:222
  125.3 1.4 copy-start.6
  126.7 0.8 copy-start.8
  128.7 27.1 %all-to-all-start = ((bf16[4,192,768]{2,1,0:T(8,128)(2,1)}), bf16[4,192,768]{2,1,0:T(8,128)(2,1)S(1)}, u32[]{:S(2)}, u32[]{:S(2)}) async-start(bf16[4,192,768]{2,1,0:T(8,128)(2,1)} %broadcast_in_dim.19), calls=%async_computation | async-start | bytes 2359296 | tf_op jit(solution)/shard_map/all_to_all | solution.py:279
  132.2 1.7 copy-start.7
  133.9 1.1 copy-start.9
  153.8 1.0 copy-start.2
  154.8 1.0 copy-start.4
  155.8 1.7 copy-start.1
  157.5 1.3 copy-start.3
  158.7 1.3 copy-start.5
Sparse Core Ops, SparseCore 0:
  62.9 69.8 all-gather.1

commit v3 on v2

--- a/solution.py
+++ b/solution.py
@@ -77,16 +77,40 @@
 
 BANDS = STEPS // 2
 FOLD = (STEPS + 1) * B
+FOLD_ROWS = BANDS * B
 SPLIT = 3
 CUT = SPLIT * B
 
 
-def fold(a):
-    bands = []
-    for k in range(BANDS):
-        j = STEPS - 1 - k
-        bands.append(jnp.concatenate([a[k * B : (k + 1) * B, k * B :], a[j * B : (j + 1) * B, j * B :]], axis=1))
-    return jnp.concatenate(bands, axis=0)
+def prepare_kernel(where_ref, cov_ref, low_ref, high_ref, rows_low_ref, rows_high_ref):
+    row, col = where_ref[0], where_ref[1]
+    own = jnp.logical_and(row == 0, col == 0)
+    zero = jnp.zeros((), cov_ref.dtype)
+    half = FOLD_ROWS // 2
+    for k in range(STEPS):
+        j = min(k, STEPS - 1 - k)
+        at = slice(0, N - k * B) if j == k else slice(N - j * B, FOLD)
+        for first in range(0, B, B // 2):
+            to = j * B + first
+            ref, to = (low_ref, to) if to < half else (high_ref, to - half)
+            rows = slice(k * B + first, k * B + first + B // 2)
+            ref[to : to + B // 2, at] = jnp.where(own, cov_ref[rows, k * B : N], zero)
+    rows_low_ref[...] = jnp.where(col == 0, cov_ref[: N // 2, :N], zero)
+    rows_high_ref[...] = jnp.where(col == 0, cov_ref[N // 2 :, :N], zero)
+
+
+def prepare(place, cov):
+    vm = pl.BlockSpec(memory_space=pltpu.VMEM)
+    folded = pltpu.VMEM((FOLD_ROWS // 2, FOLD), cov.dtype)
+    rows = pltpu.HBM((N // 2, N), cov.dtype)
+    return pl.pallas_call(
+        prepare_kernel,
+        out_shape=[folded, folded, rows, rows],
+        in_specs=[pl.BlockSpec(memory_space=pltpu.SMEM), vm],
+        out_specs=[vm, vm, vm, vm],
+        compiler_params=pltpu.CompilerParams(vmem_limit_bytes=16 << 20),
+        name="prepare",
+    )(place, cov)
 
 
 def eliminate(k, s_ref, w_ref, base):
@@ -105,7 +129,15 @@
             w_ref[a:b, :hi] = w_ref[a:b, :hi] - mm_t(uq, w_ref[lo:hi, :hi])
 
 
-def first_kernel(a_ref, s_out, w_ref, s_ref):
+def write_out(pairs, sem):
+    copies = [pltpu.make_async_copy(src, dst, sem.at[i]) for i, (src, dst) in enumerate(pairs)]
+    for copy in copies:
+        copy.start()
+    for copy in copies:
+        copy.wait()
+
+
+def first_kernel(a_ref, s_out, w_out, s_ref, w_ref, sem):
     for k in range(BANDS):
         band = a_ref[k * B : (k + 1) * B, :].astype(jnp.float32)
         j = STEPS - 1 - k
@@ -114,10 +146,10 @@
     w_ref[...] = jnp.zeros_like(w_ref)
     for k in range(SPLIT):
         eliminate(k, s_ref, w_ref, 0)
-    s_out[...] = s_ref[CUT:, CUT:]
-
-
-def second_kernel(s_in, w_in, hi_ref, lo_ref, s_ref, w_ref):
+    write_out([(s_ref.at[CUT:, CUT:], s_out), (w_ref, w_out)], sem)
+
+
+def second_kernel(s_in, w_in, hi_out, lo_out, s_ref, w_ref, hi_ref, lo_ref, sem):
     s_ref[...] = s_in[...]
     w_ref[...] = w_in[...]
     for k in range(SPLIT, STEPS):
@@ -126,30 +158,34 @@
     high = w.astype(jnp.bfloat16)
     hi_ref[...] = high
     lo_ref[...] = (w - high.astype(jnp.float32)).astype(jnp.bfloat16)
+    write_out([(hi_ref, hi_out), (lo_ref, lo_out)], sem)
 
 
 def factor(folded):
     vm = pl.BlockSpec(memory_space=pltpu.VMEM)
+    hbm = pl.BlockSpec(memory_space=pltpu.HBM)
+    sems = pltpu.SemaphoreType.DMA((2,))
+    low = pltpu.VMEM((N, N), jnp.bfloat16)
     f32 = jnp.float32
     cost = pl.CostEstimate(flops=20_000_000_000, bytes_accessed=4_000_000, transcendentals=0)
     params = pltpu.CompilerParams(vmem_limit_bytes=16 << 20)
     rest = N - CUT
     state = pl.pallas_call(
         first_kernel,
-        out_shape=[jax.ShapeDtypeStruct((rest, rest), f32), jax.ShapeDtypeStruct((N, N), f32)],
+        out_shape=[pltpu.HBM((rest, rest), f32), pltpu.HBM((N, N), f32)],
         in_specs=[vm],
-        out_specs=[vm, vm],
-        scratch_shapes=[pltpu.VMEM((N, N), f32)],
+        out_specs=[hbm, hbm],
+        scratch_shapes=[pltpu.VMEM((N, N), f32), pltpu.VMEM((N, N), f32), sems],
         compiler_params=params,
         cost_estimate=cost,
         name="factor_first",
     )(folded)
     return state, lambda s, w: pl.pallas_call(
         second_kernel,
-        out_shape=[jax.ShapeDtypeStruct((N, N), jnp.bfloat16)] * 2,
+        out_shape=[pltpu.HBM((N, N), jnp.bfloat16)] * 2,
         in_specs=[vm, vm],
-        out_specs=[vm, vm],
-        scratch_shapes=[pltpu.VMEM((rest, rest), f32), pltpu.VMEM((N, N), f32)],
+        out_specs=[hbm, hbm],
+        scratch_shapes=[pltpu.VMEM((rest, rest), f32), pltpu.VMEM((N, N), f32), low, low, sems],
         compiler_params=params,
         cost_estimate=cost,
         name="factor_second",
@@ -232,51 +268,72 @@
     ]
 
 
-def fan(x, sources, offsets, cores=(0,)):
-    return sum([send(x, shifts(sources, by, cores)) for by in offsets], x)
-
-
-def scatter(x, size, sources, offsets, cores=(0,)):
-    sent = [
-        send(x[i * size : (i + 1) * size], shifts(sources, by, cores)) for i, by in enumerate(offsets, 1)
-    ]
-    return sum(sent, x[:size])
+def halve(low, high, sources, by, cores=(0,)):
+    return low + send(high, shifts(sources, by, cores))
+
+
+def halves(x):
+    return x[: x.shape[0] // 2], x[x.shape[0] // 2 :]
+
+
+def double(x, sources, by, cores=(0,)):
+    return x + send(x, shifts(sources, by, cores))
+
+
+def other_core(x):
+    return x + lax.ppermute(x, "row", [(2 * chip, 2 * chip + 1) for chip in range(16)])
+
+
+def gather(x, axis, groups):
+    copies = jnp.broadcast_to(x[None], (4, *x.shape)).reshape(4 * x.shape[0], x.shape[1])
+    return lax.all_to_all(copies, axis, 0, 0, axis_index_groups=groups, tiled=True)
+
+
+SAME_X = [[8 * x + i for x in range(4)] for i in range(8)]
+SAME_Z = [[8 * y + odd + 2 * z for z in range(4)] for y in range(2) for odd in range(2)]
 
 
 def per_device(covariance):
     row = lax.axis_index("row")
     col = lax.axis_index("col")
     place = jnp.stack([row, col]).astype(jnp.int32)
-
-    leading = jnp.where(jnp.logical_and(row == 0, col == 0), fold(covariance[:, :N]), 0)
-    along_x = [(1, 0, 0), (2, 0, 0), (3, 0, 0)]
-    leading = scatter(leading, leading.shape[0] // 4, [(0, 0, 0)], along_x)
-    leading = fan(leading, chips(range(4), [0], [0]), [(0, 0, 4), (0, 0, 2), (0, 0, 6)])
-    leading = fan(leading, chips(range(4), [0], range(0, 8, 2)), [(0, 4, 1), (0, 4, 0), (0, 0, 1)])
-    leading = fan(leading, chips(range(4), [0, 4], range(8)), [(0, 2, 0), (0, 1, 0), (0, 7, 0)])
-    leading = leading + lax.ppermute(leading, "row", [(2 * chip, 2 * chip + 1) for chip in range(16)])
-    same_x = [[8 * x + i for x in range(4)] for i in range(8)]
-    leading = lax.all_gather(leading, "row", axis=0, tiled=True, axis_index_groups=same_x)
-
-    columns = chips([0], [0, 4], range(8))
-    cols = jnp.where(row == 0, covariance, 0)
-    cols = scatter(cols, PART, columns, along_x)
-    cols = scatter(cols, PART // 4, chips(range(4), [0, 4], range(8)), [(0, 1, 0), (0, 2, 0), (0, 3, 0)])
-    half = cols.shape[0] // 2
-    other = lax.ppermute(cols[half:], "row", [(2 * chip, 2 * chip + 1) for chip in range(16)])
-    cols = jnp.where(row % 2 == 0, cols[:half], other)
-    cols = lax.all_gather(cols, "row", axis=0, tiled=True)
-
     both = (0, 1)
-    rows = jnp.where(col == 0, covariance[:, :N], 0)
-    rows = scatter(rows, PART, chips(range(4), range(4), [0]), [(0, 0, 2), (0, 0, 4), (0, 0, 6)], both)
-    rows = fan(rows, chips(range(4), range(4), range(0, 8, 2)), [(0, 0, 1)], both)
-    rows = fan(rows, chips(range(4), range(4), range(8)), [(0, 4, 0)], both)
-    same_z = [[8 * y + odd + 2 * z for z in range(4)] for y in range(2) for odd in range(2)]
-    copies = jnp.broadcast_to(rows[None], (4, *rows.shape)).reshape(N, N)
-
-    (s, w), finish = factor(leading)
-    rows = lax.all_to_all(copies, "col", 0, 0, axis_index_groups=same_z, tiled=True)
+    all_x, even_z, all_z = range(4), range(0, 8, 2), range(8)
+    low, high, rows_low, rows_high = prepare(place, covariance)
+
+    together = lambda *arrays: lax.optimization_barrier(arrays)
+    lead = halve(low, high, [(0, 0, 0)], (2, 0, 0))
+    rows = halve(rows_low, rows_high, chips(all_x, range(4), [0]), (0, 0, 4), both)
+    lead, covariance_late = together(lead, covariance)
+    cols = jnp.where(row == 0, covariance_late, 0)
+    lead = halve(*halves(lead), chips([0, 2], [0], [0]), (1, 0, 0))
+    cols = halve(*halves(cols), chips([0], [0, 4], all_z), (2, 0, 0))
+    lead = double(lead, chips(all_x, [0], [0]), (0, 4, 0))
+    lead, rows = together(lead, rows)
+    rows = halve(*halves(rows), chips(all_x, range(4), [0, 4]), (0, 0, 2), both)
+    lead = double(lead, chips(all_x, [0, 4], [0]), (0, 2, 0))
+    lead, cols = together(lead, cols)
+    cols = halve(*halves(cols), chips([0, 2], [0, 4], all_z), (1, 0, 0))
+    lead = double(lead, chips(all_x, even_z, [0]), (0, 1, 0))
+    lead, rows = together(lead, rows)
+    rows = double(rows, chips(all_x, range(4), even_z), (0, 0, 1), both)
+    lead = double(lead, chips(all_x, all_z, [0]), (0, 0, 4))
+    lead, cols = together(lead, cols)
+    cols = double(cols, chips(all_x, [0, 4], all_z), (0, 2, 0))
+    lead = double(lead, chips(all_x, all_z, [0, 4]), (0, 0, 2))
+    lead, rows = together(lead, rows)
+    rows = double(rows, chips(all_x, range(4), all_z), (0, 4, 0), both)
+    lead = double(lead, chips(all_x, all_z, even_z), (0, 0, 1))
+    lead, cols = together(lead, cols)
+    cols = double(cols, chips(all_x, [0, 2, 4, 6], all_z), (0, 1, 0))
+    lead = gather(other_core(lead), "row", SAME_X)
+    lead, cols = together(lead, cols)
+    cols = other_core(cols)
+
+    (s, w), finish = factor(lead)
+    s, rows, cols = together(s, rows, cols)
+    rows = gather(rows, "col", SAME_Z)
+    cols = gather(cols, "row", SAME_X)
     hi, lo = finish(s, w)
     return update(place, covariance, rows, cols, hi, lo)
 

time: 177 us -> 212 us (1.20)
  the two profiles are of different devices: /device:TPU:24 before, /device:TPU:104 now
where the time goes in v3:
time: 212 us; the launch traced here: 211 us
  waiting for transfers between devices  79.5 us (38%)
  Pallas kernels  52.6 us (25%)
  blocking collectives  33.2 us (16%)
  starting transfers between devices  28.6 us (13%)
  local copies, waits for them, and re-layouts  11 us (5%)
  other arithmetic  5.34 us (3%)
    ppermute x16, waiting for transfers between devices, send(): return lax.ppermute(x, AXES, pairs)  74.5 us
    all_to_all x1, blocking collectives, gather(): lax.all_to_all(copies, axis, 0, 0, axis_index_groups=groups, tiled=True)  33.2 us
    pallas_call x1, Pallas kernels, factor(): pl.pallas_call(first_kernel, out_shape=[pltpu.HBM((rest, rest), f32), plt...  21.6 us
    pallas_call x1, Pallas kernels, factor(): pl.pallas_call(second_kernel, out_shape=[pltpu.HBM((N, N), jnp.bfloat16)]...  19.9 us
    ppermute x16, starting transfers between devices, send(): return lax.ppermute(x, AXES, pairs)  12.9 us
    all_to_all x2, starting transfers between devices, gather(): lax.all_to_all(copies, axis, 0, 0, axis_index_groups=groups, tiled=True)  12.2 us
    pallas_call x1, Pallas kernels, update(): pl.pallas_call(update_kernel, out_shape=jax.ShapeDtypeStruct(cov.shape, j...  9.36 us
    unnamed x22, local copies, waits for them, and re-layouts  8.7 us
  transfers between devices with their start and end apart: 20, of which 3 were waited for; matrix products, arithmetic and copies ran while one was open for 2% of the time, Pallas kernels for 20%

profile of v3, /device:TPU:104, one launch (start us, length us, event | category | flops | bytes accessed | tf_op | source)
XLA Modules:
  0.0 210.7 jit_solution(14945003641813019724)
XLA Ops:
  0.0 0.1 pad_add_fusion.where_ref
  0.1 1.7 copy-done
  1.7 1.7 prepare.1
  3.5 0.7 collective-permute-start
  4.1 0.1 add.54
  4.2 0.2 broadcast_select_fusion
  4.4 0.1 slice.33
  4.5 0.9 collective-permute-start.5
  5.4 0.1 copy-done.10
  5.5 0.7 collective-permute-start.3
  6.2 0.7 collective-permute-start.1
  6.9 0.7 collective-permute-start.2
  7.6 0.1 add.57
  7.8 0.7 collective-permute-start.4
  8.5 0.7 collective-permute-start.7
  9.3 0.2 slice_add_fusion
  9.5 0.7 collective-permute-start.9
  10.2 0.7 collective-permute-start.6
  11.0 0.7 collective-permute-start.8
  11.8 0.7 collective-permute-start.13
  12.5 0.7 collective-permute-start.11
  13.2 0.7 collective-permute-start.10
  14.1 1.3 collective-permute-start.12
  15.4 55.5 %collective-permute-done.12 = bf16[96,896]{1,0:T(8,128)(2,1)S(1)} collective-permute-done((bf16[96,896]{1,0:T(8,128)(2,1)S(1)}, bf16[96,896]{1,0:T(8,128)(2,1)S(1)}, u32[]{:S(2)}, u32[]{:S(2)}) %collective-permute-start.12) | collective-permute-done | bytes 172064 | tf_op jit(solution)/shard_map/ppermute | solution.py:258
  71.0 1.0 add.67
  72.0 1.3 collective-permute-start.14
  73.3 1.3 collective-permute-start.15
  74.7 0.9 broadcast_in_dim.11
  75.6 3.5 %all-to-all-start = ((bf16[4,96,896]{2,1,0:T(8,128)(2,1)}), bf16[4,96,896]{2,1,0:T(8,128)(2,1)S(1)}, u32[]{:S(2)}, u32[]{:S(2)}) async-start(bf16[4,96,896]{2,1,0:T(8,128)(2,1)} %broadcast_in_dim.11), calls=%async_computation | async-start | bytes 1376256 | tf_op jit(solution)/shard_map/all_to_all | solution.py:289
  79.1 1.3 collective-permute-start.16
  80.4 18.9 %collective-permute-done.16 = bf16[192,768]{1,0:T(8,128)(2,1)S(1)} collective-permute-done((bf16[192,768]{1,0:T(8,128)(2,1)S(1)}, bf16[192,768]{1,0:T(8,128)(2,1)S(1)}, u32[]{:S(2)}, u32[]{:S(2)}) %collective-permute-start.16) | collective-permute-done | bytes 294944 | tf_op jit(solution)/shard_map/ppermute | solution.py:258
  99.2 0.8 add.70
  100.0 2.2 %add.69 = bf16[192,1536]{1,0:T(8,128)(2,1)} add(bf16[192,1536]{1,0:T(8,128)(2,1)} %add.67, bf16[192,1536]{1,0:T(8,128)(2,1)} %collective-permute-done.15) | non-fusion elementwise | flops 294912 | bytes 1769472 | tf_op jit(solution)/shard_map/add | solution.py:280
  102.3 2.3 %collective-permute-start.17 = (bf16[192,1536]{1,0:T(8,128)(2,1)}, bf16[192,1536]{1,0:T(8,128)(2,1)S(1)}, u32[]{:S(2)}, u32[]{:S(2)}) collective-permute-start(bf16[192,1536]{1,0:T(8,128)(2,1)} %add.69), channel_id=1, source_target_pairs={{0,16},{32,48},{64,80},{96,112},{128,144},{160,176},{192,208},{224... | collective-permute-start | bytes 1769480 | tf_op jit(solution)/shard_map/ppermute | solution.py:284
  104.6 21.6 %factor_first.1 = (f32[384,384]{1,0:T(8,128)}, f32[768,768]{1,0:T(8,128)}) custom-call(bf16[384,896]{1,0:T(8,128)(2,1)S(1)} %bitcast.7), custom_call_target="tpu_custom_call" | custom-call | flops 20000000000 | bytes 4000000 | tf_op jit(solution)/shard_map/factor_first/pallas_call | solution.py:173
  126.2 0.1 add.71
  126.3 0.2 broadcast_in_dim.13
  126.5 33.2 %all_to_all.25 = bf16[4,192,1536]{2,1,0:T(8,128)(2,1)} all-to-all(bf16[4,192,1536]{2,1,0:T(8,128)(2,1)S(1)} %broadcast_in_dim.13), channel_id=1, replica_groups={{0,128,256,384},{16,144,272,400},{32,160,288,416},{48,176,304,432},{64,..., dimensions={0} | all-to-all | bytes 4718592 | tf_op jit(solution)/shard_map/all_to_all | solution.py:289
  159.7 1.1 broadcast_in_dim.12
  160.8 8.7 %all-to-all-start.1 = ((bf16[4,192,768]{2,1,0:T(8,128)(2,1)}), bf16[4,192,768]{2,1,0:T(8,128)(2,1)S(1)}, u32[]{:S(2)}, u32[]{:S(2)}) async-start(bf16[4,192,768]{2,1,0:T(8,128)(2,1)} %broadcast_in_dim.12), calls=%async_computation.1 | async-start | bytes 2359296 | tf_op jit(solution)/shard_map/all_to_all | solution.py:289
  169.5 1.7 copy-done.5
  171.1 1.1 copy-done.6
  172.2 19.9 %factor_second.1 = (bf16[768,768]{1,0:T(8,128)(2,1)}, bf16[768,768]{1,0:T(8,128)(2,1)}) custom-call(f32[384,384]{1,0:T(8,128)S(1)} %copy-done.6, f32[768,768]{1,0:T(8,128)S(1)} %copy-done.5), custom_call_target="tpu_custom_call" | custom-call | flops 20000000000 | bytes 4000000 | tf_op jit(solution)/shard_map/factor_second/pallas_call | solution.py:183
  192.1 5.0 %all-to-all-done.1 = bf16[4,192,768]{2,1,0:T(8,128)(2,1)S(1)} async-done(((bf16[4,192,768]{2,1,0:T(8,128)(2,1)}), bf16[4,192,768]{2,1,0:T(8,128)(2,1)S(1)}, u32[]{:S(2)}, u32[]{:S(2)}) %all-to-all-start.1) | async-done | bytes 1179680 | tf_op jit(solution)/shard_map/all_to_all | solution.py:289
  197.1 1.7 copy-done.2
  198.8 1.3 copy-done.3
  200.1 1.3 copy-done.4
  201.3 9.4 %update.1 = bf16[768,1536]{1,0:T(8,128)(2,1)} custom-call(s32[2]{0:T(128)S(1)} %pad_add_fusion.where_ref, bf16[768,1536]{1,0:T(8,128)(2,1)S(1)} %copy-done.1, bf16[768,768]{1,0:T(8,128)(2,1)S(1)} %bitcast.6, bf16[768,1536]{1,0:T(8,128)(2,1)S(1)} %bitcast.5, bf16[768,768]{1,0:T(8,128)(2,1)S(1)} %copy-done.3, bf16[768,768]{1,0:T(8,128)(2,1)S(1)} %copy-done.4), custom_call_target="tpu_custom_call" | custom-call | tf_op jit(solution)/shard_map/update/pallas_call | solution.py:236
  (46 shorter events, 0.7 us)
Async XLA Ops:
  0.1 1.7 copy-start
  1.7 2.5 %copy-start.1 = (bf16[768,1536]{1,0:T(8,128)(2,1)S(1)}, bf16[768,1536]{1,0:T(8,128)(2,1)}, u32[]{:S(2)}) copy-start(bf16[768,1536]{1,0:T(8,128)(2,1)} %cov_ref.3) | copy-start | bytes 7077892
  3.5 0.7 collective-permute-start
  4.4 1.1 copy-start.10
  4.4 3.2 %copy-start.9 = (bf16[384,768]{1,0:T(8,128)(2,1)S(1)}, bf16[384,768]{1,0:T(8,128)(2,1)}, u32[]{:S(2)}) copy-start(bf16[384,768]{1,0:T(8,128)(2,1)} %get-tuple-element.35) | copy-start | bytes 1769476
  4.5 4.8 %collective-permute-start.5 = (bf16[384,1536]{1,0:T(8,128)(2,1)S(1)}, bf16[384,1536]{1,0:T(8,128)(2,1)S(1)}, u32[]{:S(2)}, u32[]{:S(2)}) collective-permute-start(bf16[384,1536]{1,0:T(8,128)(2,1)S(1)} %slice.33), channel_id=1, source_target_pairs={{0,256},{1,257},{2,258},{3,259},{4,260},{5,261},{6,262},{7,263},{8... | collective-permute-start | bytes 3538952 | tf_op jit(solution)/shard_map/ppermute | solution.py:258
  5.5 2.1 %collective-permute-start.3 = (bf16[384,768]{1,0:T(8,128)(2,1)S(1)}, bf16[384,768]{1,0:T(8,128)(2,1)S(1)}, u32[]{:S(2)}, u32[]{:S(2)}) collective-permute-start(bf16[384,768]{1,0:T(8,128)(2,1)S(1)} %copy-done.10), channel_id=1, source_target_pairs={{0,4},{16,20},{32,36},{48,52},{64,68},{80,84},{96,100},{112,116},{... | collective-permute-start | bytes 1769480 | tf_op jit(solution)/shard_map/ppermute | solution.py:258
  6.2 0.7 collective-permute-start.1
  6.9 0.8 collective-permute-start.2
  7.8 1.4 collective-permute-start.4
  8.5 2.4 %collective-permute-start.7 = (bf16[192,768]{1,0:T(8,128)(2,1)S(1)}, bf16[192,768]{1,0:T(8,128)(2,1)S(1)}, u32[]{:S(2)}, u32[]{:S(2)}) collective-permute-start(bf16[192,768]{1,0:T(8,128)(2,1)S(1)} %slice.29), channel_id=1, source_target_pairs={{0,2},{16,18},{4,6},{20,22},{32,34},{48,50},{36,38},{52,54},{64,66... | collective-permute-start | bytes 884744 | tf_op jit(solution)/shard_map/ppermute | solution.py:258
  9.5 2.2 %collective-permute-start.9 = (bf16[192,1536]{1,0:T(8,128)(2,1)S(1)}, bf16[192,1536]{1,0:T(8,128)(2,1)S(1)}, u32[]{:S(2)}, u32[]{:S(2)}) collective-permute-start(bf16[192,1536]{1,0:T(8,128)(2,1)S(1)} %slice.31), channel_id=1, source_target_pairs={{0,128},{1,129},{2,130},{3,131},{4,132},{5,133},{6,134},{7,135},{8... | collective-permute-start | bytes 1769480 | tf_op jit(solution)/shard_map/ppermute | solution.py:258
  10.2 0.7 collective-permute-start.6
  11.0 0.7 collective-permute-start.8
  11.8 59.1 %collective-permute-start.13 = (bf16[192,1536]{1,0:T(8,128)(2,1)S(1)}, bf16[192,1536]{1,0:T(8,128)(2,1)S(1)}, u32[]{:S(2)}, u32[]{:S(2)}) collective-permute-start(bf16[192,1536]{1,0:T(8,128)(2,1)S(1)} %slice_add_fusion.1), channel_id=1, source_target_pairs={{0,64},{1,65},{2,66},{3,67},{4,68},{5,69},{6,70},{7,71},{8,72},{9,... | collective-permute-start | bytes 1769480 | tf_op jit(solution)/shard_map/ppermute | solution.py:258
  12.5 1.4 collective-permute-start.11
  13.2 0.8 collective-permute-start.10
  14.1 56.9 %collective-permute-start.12 = (bf16[96,896]{1,0:T(8,128)(2,1)S(1)}, bf16[96,896]{1,0:T(8,128)(2,1)S(1)}, u32[]{:S(2)}, u32[]{:S(2)}) collective-permute-start(bf16[96,896]{1,0:T(8,128)(2,1)S(1)} %add.64), channel_id=1, source_target_pairs={{0,1},{2,3},{4,5},{6,7},{32,33},{34,35},{36,37},{38,39},{64,65},{6... | collective-permute-start | bytes 516104 | tf_op jit(solution)/shard_map/ppermute | solution.py:258
  72.0 2.6 %collective-permute-start.14 = (bf16[96,896]{1,0:T(8,128)(2,1)S(1)}, bf16[96,896]{1,0:T(8,128)(2,1)S(1)}, u32[]{:S(2)}, u32[]{:S(2)}) collective-permute-start(bf16[96,896]{1,0:T(8,128)(2,1)S(1)} %add.66), channel_id=1, source_target_pairs={{0,16},{32,48},{64,80},{96,112},{128,144},{160,176},{192,208},{224... | collective-permute-start | bytes 516104 | tf_op jit(solution)/shard_map/ppermute | solution.py:284
  73.3 26.7 %collective-permute-start.15 = (bf16[192,1536]{1,0:T(8,128)(2,1)}, bf16[192,1536]{1,0:T(8,128)(2,1)}, u32[]{:S(2)}, u32[]{:S(2)}) collective-permute-start(bf16[192,1536]{1,0:T(8,128)(2,1)} %add.67), channel_id=1, source_target_pairs={{0,32},{1,33},{2,34},{3,35},{4,36},{5,37},{6,38},{7,39},{64,96},{6... | collective-permute-start | bytes 1769480 | tf_op jit(solution)/shard_map/ppermute | solution.py:258
  75.6 26.7 %all-to-all-start = ((bf16[4,96,896]{2,1,0:T(8,128)(2,1)}), bf16[4,96,896]{2,1,0:T(8,128)(2,1)S(1)}, u32[]{:S(2)}, u32[]{:S(2)}) async-start(bf16[4,96,896]{2,1,0:T(8,128)(2,1)} %broadcast_in_dim.11), calls=%async_computation | async-start | bytes 1376256 | tf_op jit(solution)/shard_map/all_to_all | solution.py:289
  79.1 20.2 %collective-permute-start.16 = (bf16[192,768]{1,0:T(8,128)(2,1)S(1)}, bf16[192,768]{1,0:T(8,128)(2,1)S(1)}, u32[]{:S(2)}, u32[]{:S(2)}) collective-permute-start(bf16[192,768]{1,0:T(8,128)(2,1)S(1)} %add.65), channel_id=1, source_target_pairs={{0,8},{16,24},{1,9},{17,25},{2,10},{18,26},{3,11},{19,27},{4,12},{... | collective-permute-start | bytes 884744 | tf_op jit(solution)/shard_map/ppermute | solution.py:258
  102.3 23.9 %copy-start.7 = (bf16[192,1536]{1,0:T(8,128)(2,1)S(1)}, bf16[192,1536]{1,0:T(8,128)(2,1)}, u32[]{:S(2)}) copy-start(bf16[192,1536]{1,0:T(8,128)(2,1)} %add.69) | copy-start | bytes 1769476
  102.3 23.9 %collective-permute-start.17 = (bf16[192,1536]{1,0:T(8,128)(2,1)}, bf16[192,1536]{1,0:T(8,128)(2,1)S(1)}, u32[]{:S(2)}, u32[]{:S(2)}) collective-permute-start(bf16[192,1536]{1,0:T(8,128)(2,1)} %add.69), channel_id=1, source_target_pairs={{0,16},{32,48},{64,80},{96,112},{128,144},{160,176},{192,208},{224... | collective-permute-start | bytes 1769480 | tf_op jit(solution)/shard_map/ppermute | solution.py:284
  126.5 33.2 %copy-start.8 = (bf16[192,768]{1,0:T(8,128)(2,1)S(1)}, bf16[192,768]{1,0:T(8,128)(2,1)}, u32[]{:S(2)}) copy-start(bf16[192,768]{1,0:T(8,128)(2,1)} %add.70) | copy-start | bytes 884740
  160.8 36.3 %all-to-all-start.1 = ((bf16[4,192,768]{2,1,0:T(8,128)(2,1)}), bf16[4,192,768]{2,1,0:T(8,128)(2,1)S(1)}, u32[]{:S(2)}, u32[]{:S(2)}) async-start(bf16[4,192,768]{2,1,0:T(8,128)(2,1)} %broadcast_in_dim.12), calls=%async_computation.1 | async-start | bytes 2359296 | tf_op jit(solution)/shard_map/all_to_all | solution.py:289
  169.5 1.7 copy-start.5
  171.1 1.1 copy-start.6
  197.1 1.7 copy-start.2
  198.8 1.3 copy-start.3
  200.1 1.3 copy-start.4

commit v4 on v3

--- a/solution.py
+++ b/solution.py
@@ -78,8 +78,6 @@
 BANDS = STEPS // 2
 FOLD = (STEPS + 1) * B
 FOLD_ROWS = BANDS * B
-SPLIT = 3
-CUT = SPLIT * B
 
 
 def prepare_kernel(where_ref, cov_ref, low_ref, high_ref, rows_low_ref, rows_high_ref):
@@ -137,23 +135,15 @@
         copy.wait()
 
 
-def first_kernel(a_ref, s_out, w_out, s_ref, w_ref, sem):
+def factor_kernel(a_ref, hi_out, lo_out, s_ref, w_ref, hi_ref, lo_ref, sem):
     for k in range(BANDS):
         band = a_ref[k * B : (k + 1) * B, :].astype(jnp.float32)
         j = STEPS - 1 - k
         s_ref[k * B : (k + 1) * B, k * B :] = band[:, : N - k * B]
         s_ref[j * B : (j + 1) * B, j * B :] = band[:, N - k * B :]
     w_ref[...] = jnp.zeros_like(w_ref)
-    for k in range(SPLIT):
+    for k in range(STEPS):
         eliminate(k, s_ref, w_ref, 0)
-    write_out([(s_ref.at[CUT:, CUT:], s_out), (w_ref, w_out)], sem)
-
-
-def second_kernel(s_in, w_in, hi_out, lo_out, s_ref, w_ref, hi_ref, lo_ref, sem):
-    s_ref[...] = s_in[...]
-    w_ref[...] = w_in[...]
-    for k in range(SPLIT, STEPS):
-        eliminate(k, s_ref, w_ref, CUT)
     w = w_ref[...]
     high = w.astype(jnp.bfloat16)
     hi_ref[...] = high
@@ -164,32 +154,17 @@
 def factor(folded):
     vm = pl.BlockSpec(memory_space=pltpu.VMEM)
     hbm = pl.BlockSpec(memory_space=pltpu.HBM)
-    sems = pltpu.SemaphoreType.DMA((2,))
-    low = pltpu.VMEM((N, N), jnp.bfloat16)
-    f32 = jnp.float32
-    cost = pl.CostEstimate(flops=20_000_000_000, bytes_accessed=4_000_000, transcendentals=0)
-    params = pltpu.CompilerParams(vmem_limit_bytes=16 << 20)
-    rest = N - CUT
-    state = pl.pallas_call(
-        first_kernel,
-        out_shape=[pltpu.HBM((rest, rest), f32), pltpu.HBM((N, N), f32)],
+    f32, low = pltpu.VMEM((N, N), jnp.float32), pltpu.VMEM((N, N), jnp.bfloat16)
+    return pl.pallas_call(
+        factor_kernel,
+        out_shape=[pltpu.HBM((N, N), jnp.bfloat16)] * 2,
         in_specs=[vm],
         out_specs=[hbm, hbm],
-        scratch_shapes=[pltpu.VMEM((N, N), f32), pltpu.VMEM((N, N), f32), sems],
-        compiler_params=params,
-        cost_estimate=cost,
-        name="factor_first",
+        scratch_shapes=[f32, f32, low, low, pltpu.SemaphoreType.DMA((2,))],
+        compiler_params=pltpu.CompilerParams(vmem_limit_bytes=16 << 20),
+        cost_estimate=pl.CostEstimate(flops=40_000_000_000, bytes_accessed=4_000_000, transcendentals=0),
+        name="factor",
     )(folded)
-    return state, lambda s, w: pl.pallas_call(
-        second_kernel,
-        out_shape=[pltpu.HBM((N, N), jnp.bfloat16)] * 2,
-        in_specs=[vm, vm],
-        out_specs=[hbm, hbm],
-        scratch_shapes=[pltpu.VMEM((rest, rest), f32), pltpu.VMEM((N, N), f32), low, low, sems],
-        compiler_params=params,
-        cost_estimate=cost,
-        name="factor_second",
-    )(s, w)
 
 
 TILE = 256
@@ -280,10 +255,6 @@
     return x + send(x, shifts(sources, by, cores))
 
 
-def other_core(x):
-    return x + lax.ppermute(x, "row", [(2 * chip, 2 * chip + 1) for chip in range(16)])
-
-
 def gather(x, axis, groups):
     copies = jnp.broadcast_to(x[None], (4, *x.shape)).reshape(4 * x.shape[0], x.shape[1])
     return lax.all_to_all(copies, axis, 0, 0, axis_index_groups=groups, tiled=True)
@@ -304,37 +275,38 @@
     together = lambda *arrays: lax.optimization_barrier(arrays)
     lead = halve(low, high, [(0, 0, 0)], (2, 0, 0))
     rows = halve(rows_low, rows_high, chips(all_x, range(4), [0]), (0, 0, 4), both)
+    lead = halve(*halves(lead), chips([0, 2], [0], [0]), (1, 0, 0))
     lead, covariance_late = together(lead, covariance)
     cols = jnp.where(row == 0, covariance_late, 0)
-    lead = halve(*halves(lead), chips([0, 2], [0], [0]), (1, 0, 0))
     cols = halve(*halves(cols), chips([0], [0, 4], all_z), (2, 0, 0))
     lead = double(lead, chips(all_x, [0], [0]), (0, 4, 0))
     lead, rows = together(lead, rows)
     rows = halve(*halves(rows), chips(all_x, range(4), [0, 4]), (0, 0, 2), both)
     lead = double(lead, chips(all_x, [0, 4], [0]), (0, 2, 0))
+    lead = double(lead, chips(all_x, even_z, [0]), (0, 1, 0))
     lead, cols = together(lead, cols)
     cols = halve(*halves(cols), chips([0, 2], [0, 4], all_z), (1, 0, 0))
-    lead = double(lead, chips(all_x, even_z, [0]), (0, 1, 0))
     lead, rows = together(lead, rows)
     rows = double(rows, chips(all_x, range(4), even_z), (0, 0, 1), both)
     lead = double(lead, chips(all_x, all_z, [0]), (0, 0, 4))
     lead, cols = together(lead, cols)
-    cols = double(cols, chips(all_x, [0, 4], all_z), (0, 2, 0))
-    lead = double(lead, chips(all_x, all_z, [0, 4]), (0, 0, 2))
+    cols = halve(*halves(cols), chips(all_x, [0, 4], all_z), (0, 2, 0))
     lead, rows = together(lead, rows)
     rows = double(rows, chips(all_x, range(4), all_z), (0, 4, 0), both)
+    lead = double(lead, chips(all_x, all_z, [0, 4]), (0, 0, 2))
+    lead, cols = together(lead, cols)
+    cols = halve(*halves(cols), chips(all_x, even_z, all_z), (0, 1, 0))
     lead = double(lead, chips(all_x, all_z, even_z), (0, 0, 1))
     lead, cols = together(lead, cols)
-    cols = double(cols, chips(all_x, [0, 2, 4, 6], all_z), (0, 1, 0))
-    lead = gather(other_core(lead), "row", SAME_X)
-    lead, cols = together(lead, cols)
-    cols = other_core(cols)
-
-    (s, w), finish = factor(lead)
-    s, rows, cols = together(s, rows, cols)
+    kept, passed = halves(cols)
+    pairs = [(2 * chip, 2 * chip + 1) for chip in range(16)]
+    cols = jnp.where(row % 2 == 0, kept, lax.ppermute(passed, "row", pairs))
+    lead = lead + lax.ppermute(lead, "row", pairs)
+    lead, rows, cols = together(lead, rows, cols)
+    cols = lax.all_gather(cols, "row", axis=0, tiled=True)
+    lead = gather(lead, "row", SAME_X)
     rows = gather(rows, "col", SAME_Z)
-    cols = gather(cols, "row", SAME_X)
-    hi, lo = finish(s, w)
+    hi, lo = factor(lead)
     return update(place, covariance, rows, cols, hi, lo)
 
 

time: 212 us -> 174 us (0.82)
  the two profiles are of different devices: /device:TPU:104 before, /device:TPU:48 now
where the time goes in v4:
time: 174 us
  waiting for transfers between devices  55.9 us (32%)
  Pallas kernels  51.2 us (29%)
  starting transfers between devices  25.2 us (14%)
  blocking collectives  15.7 us (9%)
  between operations  13.8 us (8%)
  local copies, waits for them, and re-layouts  9.02 us (5%)
  other arithmetic  2.9 us (2%)
    ppermute x16, waiting for transfers between devices, send(): return lax.ppermute(x, AXES, pairs)  55.5 us
    pallas_call x1, Pallas kernels, factor(): pl.pallas_call(factor_kernel, out_shape=[pltpu.HBM((N, N), jnp.bfloat16)]...  40.1 us
    ppermute x16, starting transfers between devices, send(): return lax.ppermute(x, AXES, pairs)  16 us
    all_to_all x1, blocking collectives, gather(): lax.all_to_all(copies, axis, 0, 0, axis_index_groups=groups, tiled=True)  15.7 us
    pallas_call x1, Pallas kernels, update(): pl.pallas_call(update_kernel, out_shape=jax.ShapeDtypeStruct(cov.shape, j...  9.36 us
    unnamed x16, local copies, waits for them, and re-layouts  7.06 us
    all_to_all x1, starting transfers between devices, gather(): lax.all_to_all(copies, axis, 0, 0, axis_index_groups=groups, tiled=True)  6.58 us
  transfers between devices with their start and end apart: 20, of which 8 were waited for; matrix products, arithmetic and copies ran while one was open for 2% of the time, Pallas kernels for 23%

profile of v4, /device:TPU:48, one launch (start us, length us, event | category | flops | bytes accessed | tf_op | source)
XLA Modules:
  0.0 173.7 jit_solution(17791758180892963390)
XLA Ops:
  6.5 0.1 pad_add_fusion.where_ref
  6.6 1.7 copy-done
  8.3 1.7 prepare.1
  10.0 0.7 collective-permute-start
  10.7 0.1 add.55
  10.8 0.7 collective-permute-start.1
  11.5 0.2 broadcast_select_fusion
  11.7 0.1 slice.59
  11.8 0.9 collective-permute-start.6
  12.7 0.1 copy-done.7
  12.8 0.7 collective-permute-start.3
  13.5 0.7 collective-permute-start.2
  14.2 0.2 add.58
  14.4 1.3 collective-permute-start.4
  15.7 29.4 %collective-permute-done.4 = bf16[96,896]{1,0:T(8,128)(2,1)S(1)} collective-permute-done((bf16[96,896]{1,0:T(8,128)(2,1)S(1)}, bf16[96,896]{1,0:T(8,128)(2,1)S(1)}, u32[]{:S(2)}, u32[]{:S(2)}) %collective-permute-start.4) | collective-permute-done | bytes 172064 | tf_op jit(solution)/shard_map/ppermute | solution.py:233
  45.2 1.3 collective-permute-start.5
  46.5 0.7 collective-permute-start.7
  47.2 2.2 %collective-permute-done.5 = bf16[96,896]{1,0:T(8,128)(2,1)S(1)} collective-permute-done((bf16[96,896]{1,0:T(8,128)(2,1)S(1)}, bf16[96,896]{1,0:T(8,128)(2,1)S(1)}, u32[]{:S(2)}, u32[]{:S(2)}) %collective-permute-start.5) | collective-permute-done | bytes 172064 | tf_op jit(solution)/shard_map/ppermute | solution.py:233
  49.4 0.2 slice_add_fusion
  49.6 0.7 collective-permute-start.9
  50.4 1.3 collective-permute-start.8
  51.7 0.7 collective-permute-start.10
  52.4 2.2 %collective-permute-done.8 = bf16[96,896]{1,0:T(8,128)(2,1)S(1)} collective-permute-done((bf16[96,896]{1,0:T(8,128)(2,1)S(1)}, bf16[96,896]{1,0:T(8,128)(2,1)S(1)}, u32[]{:S(2)}, u32[]{:S(2)}) %collective-permute-start.8) | collective-permute-done | bytes 172064 | tf_op jit(solution)/shard_map/ppermute | solution.py:233
  54.7 1.3 collective-permute-start.12
  56.1 0.1 add.65
  56.1 1.3 collective-permute-start.11
  57.4 2.9 %collective-permute-done.11 = bf16[96,896]{1,0:T(8,128)(2,1)S(1)} collective-permute-done((bf16[96,896]{1,0:T(8,128)(2,1)S(1)}, bf16[96,896]{1,0:T(8,128)(2,1)S(1)}, u32[]{:S(2)}, u32[]{:S(2)}) %collective-permute-start.11) | collective-permute-done | bytes 172064 | tf_op jit(solution)/shard_map/ppermute | solution.py:233
  60.4 3.9 %collective-permute-done.12 = bf16[96,1536]{1,0:T(8,128)(2,1)S(1)} collective-permute-done((bf16[96,1536]{1,0:T(8,128)(2,1)S(1)}, bf16[96,1536]{1,0:T(8,128)(2,1)S(1)}, u32[]{:S(2)}, u32[]{:S(2)}) %collective-permute-start.12) | collective-permute-done | bytes 294944 | tf_op jit(solution)/shard_map/ppermute | solution.py:233
  64.3 1.3 collective-permute-start.14
  65.6 1.3 collective-permute-start.16
  66.9 1.3 collective-permute-start.13
  68.3 2.8 %collective-permute-done.13 = bf16[96,896]{1,0:T(8,128)(2,1)S(1)} collective-permute-done((bf16[96,896]{1,0:T(8,128)(2,1)S(1)}, bf16[96,896]{1,0:T(8,128)(2,1)S(1)}, u32[]{:S(2)}, u32[]{:S(2)}) %collective-permute-start.13) | collective-permute-done | bytes 172064 | tf_op jit(solution)/shard_map/ppermute | solution.py:233
  71.2 0.6 slice.55
  71.8 1.3 collective-permute-start.17
  73.1 12.0 %collective-permute-done.16 = bf16[192,768]{1,0:T(8,128)(2,1)} collective-permute-done((bf16[192,768]{1,0:T(8,128)(2,1)S(1)}, bf16[192,768]{1,0:T(8,128)(2,1)}, u32[]{:S(2)}, u32[]{:S(2)}) %collective-permute-start.16) | collective-permute-done | bytes 294944 | tf_op jit(solution)/shard_map/ppermute | solution.py:233
  85.2 1.0 add.71
  86.2 1.3 collective-permute-start.15
  87.5 0.6 slice_select_fusion
  88.2 0.4 collective-permute-done.15
  88.7 15.7 %all_to_all.16 = bf16[4,96,896]{2,1,0:T(8,128)(2,1)} all-to-all(bf16[4,96,896]{2,1,0:T(8,128)(2,1)S(1)} %broadcast_in_dim.18), channel_id=1, replica_groups={{0,128,256,384},{16,144,272,400},{32,160,288,416},{48,176,304,432},{64,..., dimensions={0} | all-to-all | bytes 1376256 | tf_op jit(solution)/shard_map/all_to_all | solution.py:260
  104.4 1.1 broadcast_in_dim.9
  105.5 6.6 %all-to-all-start = ((bf16[4,192,768]{2,1,0:T(8,128)(2,1)}), bf16[4,192,768]{2,1,0:T(8,128)(2,1)S(1)}, u32[]{:S(2)}, u32[]{:S(2)}) async-start(bf16[4,192,768]{2,1,0:T(8,128)(2,1)} %broadcast_in_dim.9), calls=%async_computation | async-start | bytes 2359296 | tf_op jit(solution)/shard_map/all_to_all | solution.py:260
  112.1 1.1 copy-done.5
  113.2 40.1 %factor.1 = (bf16[768,768]{1,0:T(8,128)(2,1)}, bf16[768,768]{1,0:T(8,128)(2,1)}) custom-call(bf16[384,896]{1,0:T(8,128)(2,1)S(1)} %bitcast.5), custom_call_target="tpu_custom_call" | custom-call | flops 40000000000 | bytes 4000000 | tf_op jit(solution)/shard_map/factor/pallas_call | solution.py:158
  153.3 1.7 copy-done.2
  155.0 1.3 copy-done.3
  156.3 1.3 copy-done.4
  157.5 9.4 %update.1 = bf16[768,1536]{1,0:T(8,128)(2,1)} custom-call(s32[2]{0:T(128)S(1)} %pad_add_fusion.where_ref, bf16[768,1536]{1,0:T(8,128)(2,1)S(1)} %copy-done.1, bf16[768,768]{1,0:T(8,128)(2,1)S(1)} %bitcast.4, bf16[768,1536]{1,0:T(8,128)(2,1)S(1)} %copy-done.2, bf16[768,768]{1,0:T(8,128)(2,1)S(1)} %copy-done.3, bf16[768,768]{1,0:T(8,128)(2,1)S(1)} %copy-done.4), custom_call_target="tpu_custom_call" | custom-call | tf_op jit(solution)/shard_map/update/pallas_call | solution.py:211
  (42 shorter events, 0.8 us)
Async XLA Ops:
  6.5 146.8 %all-gather.2.cloned.1.call-start = ((), (), s32[]{:S(2)}) async-start(), calls=%async_computation.2 | async-start | bytes 2433024 | tf_op jit(solution)/shard_map/all_gather | solution.py:306
  6.6 1.7 copy-start
  8.3 3.3 %copy-start.1 = (bf16[768,1536]{1,0:T(8,128)(2,1)S(1)}, bf16[768,1536]{1,0:T(8,128)(2,1)}, u32[]{:S(2)}) copy-start(bf16[768,1536]{1,0:T(8,128)(2,1)} %cov_ref.3) | copy-start | bytes 7077892
  10.0 0.7 collective-permute-start
  10.8 0.7 collective-permute-start.1
  11.7 1.1 copy-start.7
  11.7 2.4 %copy-start.6 = (bf16[384,768]{1,0:T(8,128)(2,1)S(1)}, bf16[384,768]{1,0:T(8,128)(2,1)}, u32[]{:S(2)}) copy-start(bf16[384,768]{1,0:T(8,128)(2,1)} %get-tuple-element.33) | copy-start | bytes 1769476
  11.8 37.6 %collective-permute-start.6 = (bf16[384,1536]{1,0:T(8,128)(2,1)S(1)}, bf16[384,1536]{1,0:T(8,128)(2,1)S(1)}, u32[]{:S(2)}, u32[]{:S(2)}) collective-permute-start(bf16[384,1536]{1,0:T(8,128)(2,1)S(1)} %slice.59), channel_id=1, source_target_pairs={{0,256},{1,257},{2,258},{3,259},{4,260},{5,261},{6,262},{7,263},{8... | collective-permute-start | bytes 3538952 | tf_op jit(solution)/shard_map/ppermute | solution.py:233
  12.8 1.4 collective-permute-start.3
  13.5 0.9 collective-permute-start.2
  14.4 30.7 %collective-permute-start.4 = (bf16[96,896]{1,0:T(8,128)(2,1)S(1)}, bf16[96,896]{1,0:T(8,128)(2,1)S(1)}, u32[]{:S(2)}, u32[]{:S(2)}) collective-permute-start(bf16[96,896]{1,0:T(8,128)(2,1)S(1)} %add.57), channel_id=1, source_target_pairs={{0,64},{8,72},{128,192},{136,200},{256,320},{264,328},{384,448},{3... | collective-permute-start | bytes 516104 | tf_op jit(solution)/shard_map/ppermute | solution.py:233
  45.2 4.2 %collective-permute-start.5 = (bf16[96,896]{1,0:T(8,128)(2,1)S(1)}, bf16[96,896]{1,0:T(8,128)(2,1)S(1)}, u32[]{:S(2)}, u32[]{:S(2)}) collective-permute-start(bf16[96,896]{1,0:T(8,128)(2,1)S(1)} %add.59), channel_id=1, source_target_pairs={{0,32},{64,96},{8,40},{72,104},{128,160},{192,224},{136,168},{200,... | collective-permute-start | bytes 516104 | tf_op jit(solution)/shard_map/ppermute | solution.py:233
  46.5 3.8 %collective-permute-start.7 = (bf16[192,768]{1,0:T(8,128)(2,1)S(1)}, bf16[192,768]{1,0:T(8,128)(2,1)S(1)}, u32[]{:S(2)}, u32[]{:S(2)}) collective-permute-start(bf16[192,768]{1,0:T(8,128)(2,1)S(1)} %slice.47), channel_id=1, source_target_pairs={{0,2},{16,18},{4,6},{20,22},{32,34},{48,50},{36,38},{52,54},{64,66... | collective-permute-start | bytes 884744 | tf_op jit(solution)/shard_map/ppermute | solution.py:233
  49.6 5.0 %collective-permute-start.9 = (bf16[192,1536]{1,0:T(8,128)(2,1)S(1)}, bf16[192,1536]{1,0:T(8,128)(2,1)S(1)}, u32[]{:S(2)}, u32[]{:S(2)}) collective-permute-start(bf16[192,1536]{1,0:T(8,128)(2,1)S(1)} %slice.49), channel_id=1, source_target_pairs={{0,128},{1,129},{2,130},{3,131},{4,132},{5,133},{6,134},{7,135},{8... | collective-permute-start | bytes 1769480 | tf_op jit(solution)/shard_map/ppermute | solution.py:233
  50.4 4.2 %collective-permute-start.8 = (bf16[96,896]{1,0:T(8,128)(2,1)S(1)}, bf16[96,896]{1,0:T(8,128)(2,1)S(1)}, u32[]{:S(2)}, u32[]{:S(2)}) collective-permute-start(bf16[96,896]{1,0:T(8,128)(2,1)S(1)} %add.60), channel_id=1, source_target_pairs={{0,4},{32,36},{64,68},{96,100},{8,12},{40,44},{72,76},{104,108},{1... | collective-permute-start | bytes 516104 | tf_op jit(solution)/shard_map/ppermute | solution.py:233
  51.7 4.4 %collective-permute-start.10 = (bf16[192,768]{1,0:T(8,128)(2,1)S(1)}, bf16[192,768]{1,0:T(8,128)(2,1)S(1)}, u32[]{:S(2)}, u32[]{:S(2)}) collective-permute-start(bf16[192,768]{1,0:T(8,128)(2,1)S(1)} %slice_add_fusion.3), channel_id=1, source_target_pairs={{0,1},{16,17},{2,3},{18,19},{4,5},{20,21},{6,7},{22,23},{32,33},{4... | collective-permute-start | bytes 884744 | tf_op jit(solution)/shard_map/ppermute | solution.py:233
  54.7 9.5 %collective-permute-start.12 = (bf16[96,1536]{1,0:T(8,128)(2,1)S(1)}, bf16[96,1536]{1,0:T(8,128)(2,1)S(1)}, u32[]{:S(2)}, u32[]{:S(2)}) collective-permute-start(bf16[96,1536]{1,0:T(8,128)(2,1)S(1)} %slice.51), channel_id=1, source_target_pairs={{0,64},{1,65},{2,66},{3,67},{4,68},{5,69},{6,70},{7,71},{8,72},{9,... | collective-permute-start | bytes 884744 | tf_op jit(solution)/shard_map/ppermute | solution.py:233
  56.1 4.2 %collective-permute-start.11 = (bf16[96,896]{1,0:T(8,128)(2,1)S(1)}, bf16[96,896]{1,0:T(8,128)(2,1)S(1)}, u32[]{:S(2)}, u32[]{:S(2)}) collective-permute-start(bf16[96,896]{1,0:T(8,128)(2,1)S(1)} %add.63), channel_id=1, source_target_pairs={{0,2},{4,6},{32,34},{36,38},{64,66},{68,70},{96,98},{100,102},{8,1... | collective-permute-start | bytes 516104 | tf_op jit(solution)/shard_map/ppermute | solution.py:233
  64.3 4.0 %collective-permute-start.14 = (bf16[48,1536]{1,0:T(8,128)(2,1)S(1)}, bf16[48,1536]{1,0:T(8,128)(2,1)S(1)}, u32[]{:S(2)}, u32[]{:S(2)}) collective-permute-start(bf16[48,1536]{1,0:T(8,128)(2,1)S(1)} %slice.53), channel_id=1, source_target_pairs={{0,32},{1,33},{2,34},{3,35},{4,36},{5,37},{6,38},{7,39},{64,96},{6... | collective-permute-start | bytes 442376 | tf_op jit(solution)/shard_map/ppermute | solution.py:233
  65.6 19.5 %collective-permute-start.16 = (bf16[192,768]{1,0:T(8,128)(2,1)S(1)}, bf16[192,768]{1,0:T(8,128)(2,1)}, u32[]{:S(2)}, u32[]{:S(2)}) collective-permute-start(bf16[192,768]{1,0:T(8,128)(2,1)S(1)} %add.65), channel_id=1, source_target_pairs={{0,8},{16,24},{1,9},{17,25},{2,10},{18,26},{3,11},{19,27},{4,12},{... | collective-permute-start | bytes 884744 | tf_op jit(solution)/shard_map/ppermute | solution.py:233
  66.9 4.2 %collective-permute-start.13 = (bf16[96,896]{1,0:T(8,128)(2,1)S(1)}, bf16[96,896]{1,0:T(8,128)(2,1)S(1)}, u32[]{:S(2)}, u32[]{:S(2)}) collective-permute-start(bf16[96,896]{1,0:T(8,128)(2,1)S(1)} %add.66), channel_id=1, source_target_pairs={{0,1},{2,3},{4,5},{6,7},{32,33},{34,35},{36,37},{38,39},{64,65},{6... | collective-permute-start | bytes 516104 | tf_op jit(solution)/shard_map/ppermute | solution.py:233
  71.8 15.7 %collective-permute-start.17 = (bf16[24,1536]{1,0:T(8,128)(2,1)}, bf16[24,1536]{1,0:T(8,128)(2,1)S(1)}, u32[]{:S(2)}, u32[]{:S(2)}) collective-permute-start(bf16[24,1536]{1,0:T(8,128)(2,1)} %slice.55), channel_id=1, source_target_pairs={{0,16},{32,48},{64,80},{96,112},{128,144},{160,176},{192,208},{224... | collective-permute-start | bytes 221192 | tf_op jit(solution)/shard_map/ppermute | solution.py:303
  86.2 2.3 %collective-permute-start.15 = (bf16[96,896]{1,0:T(8,128)(2,1)S(1)}, bf16[96,896]{1,0:T(8,128)(2,1)S(1)}, u32[]{:S(2)}, u32[]{:S(2)}) collective-permute-start(bf16[96,896]{1,0:T(8,128)(2,1)S(1)} %add.68), channel_id=1, source_target_pairs={{0,16},{32,48},{64,80},{96,112},{128,144},{160,176},{192,208},{224... | collective-permute-start | bytes 516104 | tf_op jit(solution)/shard_map/ppermute | solution.py:304
  105.5 47.8 %all-to-all-start = ((bf16[4,192,768]{2,1,0:T(8,128)(2,1)}), bf16[4,192,768]{2,1,0:T(8,128)(2,1)S(1)}, u32[]{:S(2)}, u32[]{:S(2)}) async-start(bf16[4,192,768]{2,1,0:T(8,128)(2,1)} %broadcast_in_dim.9), calls=%async_computation | async-start | bytes 2359296 | tf_op jit(solution)/shard_map/all_to_all | solution.py:260
  112.1 1.1 copy-start.5
  153.3 1.7 copy-start.2
  155.0 1.3 copy-start.3
  156.3 1.3 copy-start.4
Sparse Core Ops, SparseCore 0:
  88.7 59.6 all-gather.1

commit v5 on v4

--- a/solution.py
+++ b/solution.py
@@ -8,17 +8,25 @@
 N = 768
 B = 128
 STEPS = N // B
-HI = lax.Precision.HIGHEST
+
+
+def split(x):
+    high = x.astype(jnp.bfloat16)
+    return high, (x - high.astype(jnp.float32)).astype(jnp.bfloat16)
+
+
+def product(a, b, dim):
+    dot = lambda x, y: lax.dot_general(x, y, (((dim,), (0,)), ((), ())), preferred_element_type=jnp.float32)
+    (a_high, a_low), (b_high, b_low) = split(a), split(b)
+    return dot(a_high, b_high) + (dot(a_high, b_low) + dot(a_low, b_high))
 
 
 def mm(a, b):
-    return jnp.dot(a, b, precision=HI, preferred_element_type=jnp.float32)
+    return product(a, b, 1)
 
 
 def mm_t(a, b):
-    return lax.dot_general(
-        a, b, (((0,), (0,)), ((), ())), precision=HI, preferred_element_type=jnp.float32
-    )
+    return product(a, b, 0)
 
 
 def invert_factor(block):
@@ -247,6 +255,11 @@
     return low + send(high, shifts(sources, by, cores))
 
 
+def scatter(x, size, sources, offsets):
+    sent = [send(x[i * size : (i + 1) * size], shifts(sources, by)) for i, by in enumerate(offsets, 1)]
+    return sum(sent, x[:size])
+
+
 def halves(x):
     return x[: x.shape[0] // 2], x[x.shape[0] // 2 :]
 
@@ -262,6 +275,10 @@
 
 SAME_X = [[8 * x + i for x in range(4)] for i in range(8)]
 SAME_Z = [[8 * y + odd + 2 * z for z in range(4)] for y in range(2) for odd in range(2)]
+
+
+def in_hbm(x):
+    return pltpu.with_memory_space_constraint(x, pltpu.HBM)
 
 
 def per_device(covariance):
@@ -278,36 +295,31 @@
     lead = halve(*halves(lead), chips([0, 2], [0], [0]), (1, 0, 0))
     lead, covariance_late = together(lead, covariance)
     cols = jnp.where(row == 0, covariance_late, 0)
-    cols = halve(*halves(cols), chips([0], [0, 4], all_z), (2, 0, 0))
+    cols = scatter(cols, N // 4, chips([0], [0, 4], all_z), [(1, 0, 0), (2, 0, 0), (3, 0, 0)])
     lead = double(lead, chips(all_x, [0], [0]), (0, 4, 0))
+    lead = double(lead, chips(all_x, [0, 4], [0]), (0, 2, 0))
     lead, rows = together(lead, rows)
     rows = halve(*halves(rows), chips(all_x, range(4), [0, 4]), (0, 0, 2), both)
-    lead = double(lead, chips(all_x, [0, 4], [0]), (0, 2, 0))
     lead = double(lead, chips(all_x, even_z, [0]), (0, 1, 0))
     lead, cols = together(lead, cols)
-    cols = halve(*halves(cols), chips([0, 2], [0, 4], all_z), (1, 0, 0))
-    lead, rows = together(lead, rows)
+    cols = scatter(cols, N // 16, chips(all_x, [0, 4], all_z), [(0, 1, 0), (0, 2, 0), (0, 3, 0)])
+    lead = double(lead, chips(all_x, all_z, [0]), (0, 0, 4))
+    lead, rows, cols = together(lead, rows, cols)
     rows = double(rows, chips(all_x, range(4), even_z), (0, 0, 1), both)
-    lead = double(lead, chips(all_x, all_z, [0]), (0, 0, 4))
-    lead, cols = together(lead, cols)
-    cols = halve(*halves(cols), chips(all_x, [0, 4], all_z), (0, 2, 0))
-    lead, rows = together(lead, rows)
-    rows = double(rows, chips(all_x, range(4), all_z), (0, 4, 0), both)
-    lead = double(lead, chips(all_x, all_z, [0, 4]), (0, 0, 2))
-    lead, cols = together(lead, cols)
-    cols = halve(*halves(cols), chips(all_x, even_z, all_z), (0, 1, 0))
-    lead = double(lead, chips(all_x, all_z, even_z), (0, 0, 1))
-    lead, cols = together(lead, cols)
     kept, passed = halves(cols)
     pairs = [(2 * chip, 2 * chip + 1) for chip in range(16)]
     cols = jnp.where(row % 2 == 0, kept, lax.ppermute(passed, "row", pairs))
+    lead = double(lead, chips(all_x, all_z, [0, 4]), (0, 0, 2))
+    lead, rows, cols = together(lead, rows, cols)
+    rows = double(rows, chips(all_x, range(4), all_z), (0, 4, 0), both)
+    cols = lax.all_gather(cols, "row", axis=0, tiled=True)
+    lead = double(lead, chips(all_x, all_z, even_z), (0, 0, 1))
     lead = lead + lax.ppermute(lead, "row", pairs)
-    lead, rows, cols = together(lead, rows, cols)
-    cols = lax.all_gather(cols, "row", axis=0, tiled=True)
+    lead, rows = together(lead, rows)
     lead = gather(lead, "row", SAME_X)
     rows = gather(rows, "col", SAME_Z)
-    hi, lo = factor(lead)
-    return update(place, covariance, rows, cols, hi, lo)
+    hi, lo = factor(in_hbm(lead))
+    return update(place, in_hbm(covariance), rows, in_hbm(cols), in_hbm(hi), in_hbm(lo))
 
 
 def solution(mesh):

time: 174 us -> 163 us (0.937)
  Pallas kernels: 51.2 us -> 44.7 us
  local copies, waits for them, and re-layouts: 9.02 us -> 3.69 us
  waiting for transfers between devices: 55.9 us -> 59.6 us
  starting transfers between devices: 25.2 us -> 23 us
    pallas_call x1, Pallas kernels: 40.1 us -> 32 us  [factor(): pl.pallas_call(factor_kernel, out_shape=[pltpu.HBM((N, N), jnp.bfloat16)]...]
    unnamed x16 -> x6, local copies, waits for them, and re-layouts: 7.06 us -> 1.67 us
    ppermute x16 -> x18, waiting for transfers between devices: 55.5 us -> 59.6 us  [send(): return lax.ppermute(x, AXES, pairs)]
    all_to_all x1, starting transfers between devices: 6.58 us -> 3.71 us  [gather(): lax.all_to_all(copies, axis, 0, 0, axis_index_groups=groups, tiled=True)]
    ppermute x16 -> x18, starting transfers between devices: 16 us -> 16.7 us  [send(): return lax.ppermute(x, AXES, pairs)]
  transfers between devices with their start and end apart: 20 -> 22, of which waited for: 8 -> 6; matrix products, arithmetic and copies ran while one was open for 2% -> 2% of each run, Pallas kernels for 23% -> 20%
where the time goes in v5:
time: 163 us
  waiting for transfers between devices  59.6 us (37%)
  Pallas kernels  44.7 us (27%)
  starting transfers between devices  23 us (14%)
  blocking collectives  16 us (10%)
  between operations  13.9 us (9%)
  local copies, waits for them, and re-layouts  3.69 us (2%)
  other arithmetic  1.8 us (1%)
    ppermute x18, waiting for transfers between devices, send(): return lax.ppermute(x, AXES, pairs)  59.6 us
    pallas_call x1, Pallas kernels, factor(): pl.pallas_call(factor_kernel, out_shape=[pltpu.HBM((N, N), jnp.bfloat16)]...  32 us
    ppermute x18, starting transfers between devices, send(): return lax.ppermute(x, AXES, pairs)  16.7 us
    all_to_all x1, blocking collectives, gather(): lax.all_to_all(copies, axis, 0, 0, axis_index_groups=groups, tiled=True)  16 us
    pallas_call x1, Pallas kernels, update(): pl.pallas_call(update_kernel, out_shape=jax.ShapeDtypeStruct(cov.shape, j...  10.9 us
    all_to_all x1, starting transfers between devices, gather(): lax.all_to_all(copies, axis, 0, 0, axis_index_groups=groups, tiled=True)  3.71 us
  transfers between devices with their start and end apart: 22, of which 6 were waited for; matrix products, arithmetic and copies ran while one was open for 2% of the time, Pallas kernels for 20%

profile of v5, /device:TPU:48, one launch (start us, length us, event | category | flops | bytes accessed | tf_op | source)
XLA Modules:
  0.0 162.6 jit_solution(7805452653518906129)
XLA Ops:
  6.5 0.1 pad_add_fusion.where_ref
  6.6 1.7 %copy-done = bf16[768,1536]{1,0:T(8,128)(2,1)S(1)} copy-done((bf16[768,1536]{1,0:T(8,128)(2,1)S(1)}, bf16[768,1536]{1,0:T(8,128)(2,1)}, u32[]{:S(2)}) %copy-start) | copy-done | bytes 2359320
  8.3 1.7 %prepare.1 = (bf16[192,896]{1,0:T(8,128)(2,1)S(1)}, bf16[192,896]{1,0:T(8,128)(2,1)S(1)}, bf16[384,768]{1,0:T(8,128)(2,1)}, bf16[384,768]{1,0:T(8,128)(2,1)}) custom-call(s32[2]{0:T(128)S(1)} %pad_add_fusion.where_ref, bf16[768,1536]{1,0:T(8,128)(2,1)S(1)} %copy-done), custom_call_target="tpu_custom_call" | custom-call | tf_op jit(solution)/shard_map/prepare/pallas_call | solution.py:112
  10.0 0.7 collective-permute-start
  10.7 0.0 collective-permute-done
  10.7 0.1 add.61
  10.8 0.7 slice.57
  11.5 0.7 collective-permute-start.1
  12.1 0.7 collective-permute-start.4
  12.9 0.2 broadcast_select_fusion
  13.1 0.0 copy-start.2
  13.1 0.1 fusion.2
  13.2 0.8 collective-permute-start.6
  14.0 0.7 collective-permute-start.8
  14.7 0.7 collective-permute-start.7
  15.4 0.7 collective-permute-start.2
  16.2 1.3 collective-permute-start.3
  17.5 0.2 add.65
  17.7 30.0 %collective-permute-done.3 = bf16[96,896]{1,0:T(8,128)(2,1)S(1)} collective-permute-done((bf16[96,896]{1,0:T(8,128)(2,1)S(1)}, bf16[96,896]{1,0:T(8,128)(2,1)S(1)}, u32[]{:S(2)}, u32[]{:S(2)}) %collective-permute-start.3) | collective-permute-done | bytes 172064 | tf_op jit(solution)/shard_map/ppermute | solution.py:241
  47.7 1.3 collective-permute-start.5
  49.0 0.7 collective-permute-start.10
  49.7 2.2 %collective-permute-done.5 = bf16[96,896]{1,0:T(8,128)(2,1)S(1)} collective-permute-done((bf16[96,896]{1,0:T(8,128)(2,1)S(1)}, bf16[96,896]{1,0:T(8,128)(2,1)S(1)}, u32[]{:S(2)}, u32[]{:S(2)}) %collective-permute-start.5) | collective-permute-done | bytes 172064 | tf_op jit(solution)/shard_map/ppermute | solution.py:241
  52.0 0.1 fusion.1
  52.1 1.3 collective-permute-start.9
  53.5 0.7 collective-permute-start.11
  54.2 0.7 collective-permute-start.13
  54.8 1.3 collective-permute-start.12
  56.2 9.4 %collective-permute-done.12 = bf16[48,1536]{1,0:T(8,128)(2,1)S(1)} collective-permute-done((bf16[48,1536]{1,0:T(8,128)(2,1)S(1)}, bf16[48,1536]{1,0:T(8,128)(2,1)S(1)}, u32[]{:S(2)}, u32[]{:S(2)}) %collective-permute-start.12) | collective-permute-done | bytes 147488 | tf_op jit(solution)/shard_map/ppermute | solution.py:241
  65.7 1.3 collective-permute-start.16
  67.0 1.3 collective-permute-start.14
  68.3 0.7 collective-permute-start.15
  69.0 0.6 slice_select_fusion
  69.7 1.6 collective-permute-done.14
  71.3 0.1 add.76
  71.4 1.3 collective-permute-start.17
  72.7 0.0 all-gather.2.cloned.1.call-update
  72.7 1.3 collective-permute-start.19
  74.0 1.6 collective-permute-done.17
  75.6 1.3 collective-permute-start.18
  76.9 14.9 %collective-permute-done.19 = bf16[192,768]{1,0:T(8,128)(2,1)S(1)} collective-permute-done((bf16[192,768]{1,0:T(8,128)(2,1)S(1)}, bf16[192,768]{1,0:T(8,128)(2,1)S(1)}, u32[]{:S(2)}, u32[]{:S(2)}) %collective-permute-start.19) | collective-permute-done | bytes 294944 | tf_op jit(solution)/shard_map/ppermute | solution.py:241
  91.8 0.1 add.80
  91.9 0.1 broadcast_in_dim.18
  92.0 16.0 %all_to_all.16 = bf16[4,96,896]{2,1,0:T(8,128)(2,1)} all-to-all(bf16[4,96,896]{2,1,0:T(8,128)(2,1)S(1)} %broadcast_in_dim.18), channel_id=1, replica_groups={{0,128,256,384},{16,144,272,400},{32,160,288,416},{48,176,304,432},{64,..., dimensions={0} | all-to-all | bytes 1376256 | tf_op jit(solution)/shard_map/all_to_all | solution.py:273
  108.0 1.1 broadcast_in_dim.9
  109.1 3.7 %all-to-all-start = ((bf16[4,192,768]{2,1,0:T(8,128)(2,1)}), bf16[4,192,768]{2,1,0:T(8,128)(2,1)S(1)}, u32[]{:S(2)}, u32[]{:S(2)}) async-start(bf16[4,192,768]{2,1,0:T(8,128)(2,1)} %broadcast_in_dim.9), calls=%async_computation | async-start | bytes 2359296 | tf_op jit(solution)/shard_map/all_to_all | solution.py:273
  112.8 32.0 %factor.1 = (bf16[768,768]{1,0:T(8,128)(2,1)}, bf16[768,768]{1,0:T(8,128)(2,1)}) custom-call(bf16[384,896]{1,0:T(8,128)(2,1)} %bitcast.5), custom_call_target="tpu_custom_call" | custom-call | flops 40000000000 | bytes 4000000 | tf_op jit(solution)/shard_map/factor/pallas_call | solution.py:166
  144.8 0.0 all-gather.2.cloned.1.call-done.cols_ref
  144.8 10.9 %update.1 = bf16[768,1536]{1,0:T(8,128)(2,1)} custom-call(s32[2]{0:T(128)S(1)} %pad_add_fusion.where_ref, bf16[768,1536]{1,0:T(8,128)(2,1)} %cov_ref.3, bf16[768,768]{1,0:T(8,128)(2,1)S(1)} %bitcast.4, bf16[768,1536]{1,0:T(8,128)(2,1)} %all-gather.2.cloned.1.call-done.cols_ref, bf16[768,768]{1,0:T(8,128)(2,1)} %get-tuple-element.43.hi_ref, ...), custom_call_target="tpu_custom_call" | custom-call | tf_op jit(solution)/shard_map/update/pallas_call | solution.py:219
  (32 shorter events, 0.5 us)
Async XLA Ops:
  6.5 138.3 %all-gather.2.cloned.1.call-start = ((), (), s32[]{:S(2)}) async-start(), calls=%async_computation.2 | async-start | bytes 2433024 | tf_op jit(solution)/shard_map/all_gather | solution.py:315
  6.6 1.7 %copy-start = (bf16[768,1536]{1,0:T(8,128)(2,1)S(1)}, bf16[768,1536]{1,0:T(8,128)(2,1)}, u32[]{:S(2)}) copy-start(bf16[768,1536]{1,0:T(8,128)(2,1)} %cov_ref.3) | copy-start | bytes 7077892
  8.3 4.6 %copy-start.1 = (bf16[768,1536]{1,0:T(8,128)(2,1)S(1)}, bf16[768,1536]{1,0:T(8,128)(2,1)}, u32[]{:S(2)}) copy-start(bf16[768,1536]{1,0:T(8,128)(2,1)} %cov_ref.3) | copy-start | bytes 7077892
  10.0 0.7 collective-permute-start
  11.5 1.4 collective-permute-start.1
  12.1 5.4 %collective-permute-start.4 = (bf16[384,768]{1,0:T(8,128)(2,1)}, bf16[384,768]{1,0:T(8,128)(2,1)S(1)}, u32[]{:S(2)}, u32[]{:S(2)}) collective-permute-start(bf16[384,768]{1,0:T(8,128)(2,1)} %get-tuple-element.29), channel_id=1, source_target_pairs={{0,4},{16,20},{32,36},{48,52},{64,68},{80,84},{96,100},{112,116},{... | collective-permute-start | bytes 1769480 | tf_op jit(solution)/shard_map/ppermute | solution.py:241
  13.1 4.4 %copy-start.2 = (bf16[384,768]{1,0:T(8,128)(2,1)S(1)}, bf16[384,768]{1,0:T(8,128)(2,1)}, u32[]{:S(2)}) copy-start(bf16[384,768]{1,0:T(8,128)(2,1)} %get-tuple-element.28) | copy-start | bytes 1769476
  13.2 38.8 %collective-permute-start.6 = (bf16[192,1536]{1,0:T(8,128)(2,1)S(1)}, bf16[192,1536]{1,0:T(8,128)(2,1)S(1)}, u32[]{:S(2)}, u32[]{:S(2)}) collective-permute-start(bf16[192,1536]{1,0:T(8,128)(2,1)S(1)} %get-tuple-element.45), channel_id=1, source_target_pairs={{0,128},{1,129},{2,130},{3,131},{4,132},{5,133},{6,134},{7,135},{8... | collective-permute-start | bytes 1769480 | tf_op jit(solution)/shard_map/ppermute | solution.py:241
  14.0 37.9 %collective-permute-start.8 = (bf16[192,1536]{1,0:T(8,128)(2,1)S(1)}, bf16[192,1536]{1,0:T(8,128)(2,1)S(1)}, u32[]{:S(2)}, u32[]{:S(2)}) collective-permute-start(bf16[192,1536]{1,0:T(8,128)(2,1)S(1)} %get-tuple-element.46), channel_id=1, source_target_pairs={{0,384},{1,385},{2,386},{3,387},{4,388},{5,389},{6,390},{7,391},{8... | collective-permute-start | bytes 1769480 | tf_op jit(solution)/shard_map/ppermute | solution.py:241
  14.7 37.2 %collective-permute-start.7 = (bf16[192,1536]{1,0:T(8,128)(2,1)S(1)}, bf16[192,1536]{1,0:T(8,128)(2,1)S(1)}, u32[]{:S(2)}, u32[]{:S(2)}) collective-permute-start(bf16[192,1536]{1,0:T(8,128)(2,1)S(1)} %get-tuple-element.47), channel_id=1, source_target_pairs={{0,256},{1,257},{2,258},{3,259},{4,260},{5,261},{6,262},{7,263},{8... | collective-permute-start | bytes 1769480 | tf_op jit(solution)/shard_map/ppermute | solution.py:241
  15.4 0.7 collective-permute-start.2
  16.2 31.5 %collective-permute-start.3 = (bf16[96,896]{1,0:T(8,128)(2,1)S(1)}, bf16[96,896]{1,0:T(8,128)(2,1)S(1)}, u32[]{:S(2)}, u32[]{:S(2)}) collective-permute-start(bf16[96,896]{1,0:T(8,128)(2,1)S(1)} %add.63), channel_id=1, source_target_pairs={{0,64},{8,72},{128,192},{136,200},{256,320},{264,328},{384,448},{3... | collective-permute-start | bytes 516104 | tf_op jit(solution)/shard_map/ppermute | solution.py:241
  47.7 4.2 %collective-permute-start.5 = (bf16[96,896]{1,0:T(8,128)(2,1)S(1)}, bf16[96,896]{1,0:T(8,128)(2,1)S(1)}, u32[]{:S(2)}, u32[]{:S(2)}) collective-permute-start(bf16[96,896]{1,0:T(8,128)(2,1)S(1)} %add.64), channel_id=1, source_target_pairs={{0,32},{64,96},{8,40},{72,104},{128,160},{192,224},{136,168},{200,... | collective-permute-start | bytes 516104 | tf_op jit(solution)/shard_map/ppermute | solution.py:241
  49.0 7.1 %collective-permute-start.10 = (bf16[192,768]{1,0:T(8,128)(2,1)S(1)}, bf16[192,768]{1,0:T(8,128)(2,1)S(1)}, u32[]{:S(2)}, u32[]{:S(2)}) collective-permute-start(bf16[192,768]{1,0:T(8,128)(2,1)S(1)} %slice.49), channel_id=1, source_target_pairs={{0,2},{16,18},{4,6},{20,22},{32,34},{48,50},{36,38},{52,54},{64,66... | collective-permute-start | bytes 884744 | tf_op jit(solution)/shard_map/ppermute | solution.py:241
  52.1 13.5 %collective-permute-start.9 = (bf16[96,896]{1,0:T(8,128)(2,1)S(1)}, bf16[96,896]{1,0:T(8,128)(2,1)S(1)}, u32[]{:S(2)}, u32[]{:S(2)}) collective-permute-start(bf16[96,896]{1,0:T(8,128)(2,1)S(1)} %add.66), channel_id=1, source_target_pairs={{0,4},{32,36},{64,68},{96,100},{8,12},{40,44},{72,76},{104,108},{1... | collective-permute-start | bytes 516104 | tf_op jit(solution)/shard_map/ppermute | solution.py:241
  53.5 2.7 %collective-permute-start.11 = (bf16[48,1536]{1,0:T(8,128)(2,1)S(1)}, bf16[48,1536]{1,0:T(8,128)(2,1)S(1)}, u32[]{:S(2)}, u32[]{:S(2)}) collective-permute-start(bf16[48,1536]{1,0:T(8,128)(2,1)S(1)} %get-tuple-element.48), channel_id=1, source_target_pairs={{0,32},{1,33},{2,34},{3,35},{4,36},{5,37},{6,38},{7,39},{8,40},{9,... | collective-permute-start | bytes 442376 | tf_op jit(solution)/shard_map/ppermute | solution.py:241
  54.2 2.0 %collective-permute-start.13 = (bf16[48,1536]{1,0:T(8,128)(2,1)S(1)}, bf16[48,1536]{1,0:T(8,128)(2,1)S(1)}, u32[]{:S(2)}, u32[]{:S(2)}) collective-permute-start(bf16[48,1536]{1,0:T(8,128)(2,1)S(1)} %get-tuple-element.49), channel_id=1, source_target_pairs={{0,96},{1,97},{2,98},{3,99},{4,100},{5,101},{6,102},{7,103},{8,104... | collective-permute-start | bytes 442376 | tf_op jit(solution)/shard_map/ppermute | solution.py:241
  54.8 10.8 %collective-permute-start.12 = (bf16[48,1536]{1,0:T(8,128)(2,1)S(1)}, bf16[48,1536]{1,0:T(8,128)(2,1)S(1)}, u32[]{:S(2)}, u32[]{:S(2)}) collective-permute-start(bf16[48,1536]{1,0:T(8,128)(2,1)S(1)} %get-tuple-element.50), channel_id=1, source_target_pairs={{0,64},{1,65},{2,66},{3,67},{4,68},{5,69},{6,70},{7,71},{8,72},{9,... | collective-permute-start | bytes 442376 | tf_op jit(solution)/shard_map/ppermute | solution.py:241
  65.7 3.3 %collective-permute-start.16 = (bf16[24,1536]{1,0:T(8,128)(2,1)S(1)}, bf16[24,1536]{1,0:T(8,128)(2,1)S(1)}, u32[]{:S(2)}, u32[]{:S(2)}) collective-permute-start(bf16[24,1536]{1,0:T(8,128)(2,1)S(1)} %slice.55), channel_id=1, source_target_pairs={{0,16},{32,48},{64,80},{96,112},{128,144},{160,176},{192,208},{224... | collective-permute-start | bytes 221192 | tf_op jit(solution)/shard_map/ppermute | solution.py:311
  67.0 4.2 %collective-permute-start.14 = (bf16[96,896]{1,0:T(8,128)(2,1)S(1)}, bf16[96,896]{1,0:T(8,128)(2,1)S(1)}, u32[]{:S(2)}, u32[]{:S(2)}) collective-permute-start(bf16[96,896]{1,0:T(8,128)(2,1)S(1)} %add.70), channel_id=1, source_target_pairs={{0,2},{4,6},{32,34},{36,38},{64,66},{68,70},{96,98},{100,102},{8,1... | collective-permute-start | bytes 516104 | tf_op jit(solution)/shard_map/ppermute | solution.py:241
  68.3 2.9 %collective-permute-start.15 = (bf16[192,768]{1,0:T(8,128)(2,1)S(1)}, bf16[192,768]{1,0:T(8,128)(2,1)S(1)}, u32[]{:S(2)}, u32[]{:S(2)}) collective-permute-start(bf16[192,768]{1,0:T(8,128)(2,1)S(1)} %slice_add_fusion.1), channel_id=1, source_target_pairs={{0,1},{16,17},{2,3},{18,19},{4,5},{20,21},{6,7},{22,23},{32,33},{4... | collective-permute-start | bytes 884744 | tf_op jit(solution)/shard_map/ppermute | solution.py:241
  71.4 4.2 %collective-permute-start.17 = (bf16[96,896]{1,0:T(8,128)(2,1)S(1)}, bf16[96,896]{1,0:T(8,128)(2,1)S(1)}, u32[]{:S(2)}, u32[]{:S(2)}) collective-permute-start(bf16[96,896]{1,0:T(8,128)(2,1)S(1)} %add.75), channel_id=1, source_target_pairs={{0,1},{2,3},{4,5},{6,7},{32,33},{34,35},{36,37},{38,39},{64,65},{6... | collective-permute-start | bytes 516104 | tf_op jit(solution)/shard_map/ppermute | solution.py:241
  72.7 19.1 %collective-permute-start.19 = (bf16[192,768]{1,0:T(8,128)(2,1)S(1)}, bf16[192,768]{1,0:T(8,128)(2,1)S(1)}, u32[]{:S(2)}, u32[]{:S(2)}) collective-permute-start(bf16[192,768]{1,0:T(8,128)(2,1)S(1)} %add.76), channel_id=1, source_target_pairs={{0,8},{16,24},{1,9},{17,25},{2,10},{18,26},{3,11},{19,27},{4,12},{... | collective-permute-start | bytes 884744 | tf_op jit(solution)/shard_map/ppermute | solution.py:241
  75.6 16.3 %collective-permute-start.18 = (bf16[96,896]{1,0:T(8,128)(2,1)S(1)}, bf16[96,896]{1,0:T(8,128)(2,1)S(1)}, u32[]{:S(2)}, u32[]{:S(2)}) collective-permute-start(bf16[96,896]{1,0:T(8,128)(2,1)S(1)} %add.78), channel_id=1, source_target_pairs={{0,16},{32,48},{64,80},{96,112},{128,144},{160,176},{192,208},{224... | collective-permute-start | bytes 516104 | tf_op jit(solution)/shard_map/ppermute | solution.py:317
  109.1 35.7 %all-to-all-start = ((bf16[4,192,768]{2,1,0:T(8,128)(2,1)}), bf16[4,192,768]{2,1,0:T(8,128)(2,1)S(1)}, u32[]{:S(2)}, u32[]{:S(2)}) async-start(bf16[4,192,768]{2,1,0:T(8,128)(2,1)} %broadcast_in_dim.9), calls=%async_computation | async-start | bytes 2359296 | tf_op jit(solution)/shard_map/all_to_all | solution.py:273
Sparse Core Ops, SparseCore 0:
  72.8 59.4 all-gather.1

commit v6 on v5

--- a/solution.py
+++ b/solution.py
@@ -315,7 +315,6 @@
     cols = lax.all_gather(cols, "row", axis=0, tiled=True)
     lead = double(lead, chips(all_x, all_z, even_z), (0, 0, 1))
     lead = lead + lax.ppermute(lead, "row", pairs)
-    lead, rows = together(lead, rows)
     lead = gather(lead, "row", SAME_X)
     rows = gather(rows, "col", SAME_Z)
     hi, lo = factor(in_hbm(lead))

time: 163 us -> 163 us (level)
  the two profiles are of different devices: /device:TPU:48 before, /device:TPU:112 now
where the time goes in v6:
time: 163 us; the launch traced here: 162 us
  waiting for transfers between devices  72.1 us (44%)
  Pallas kernels  44.6 us (27%)
  starting transfers between devices  25.3 us (16%)
  between operations  13.9 us (9%)
  local copies, waits for them, and re-layouts  4.62 us (3%)
  other arithmetic  1.79 us (1%)
    ppermute x18, waiting for transfers between devices, send(): return lax.ppermute(x, AXES, pairs)  71 us
    pallas_call x1, Pallas kernels, factor(): pl.pallas_call(factor_kernel, out_shape=[pltpu.HBM((N, N), jnp.bfloat16)]...  32 us
    ppermute x18, starting transfers between devices, send(): return lax.ppermute(x, AXES, pairs)  14.2 us
    pallas_call x1, Pallas kernels, update(): pl.pallas_call(update_kernel, out_shape=jax.ShapeDtypeStruct(cov.shape, j...  10.9 us
    all_to_all x2, starting transfers between devices, gather(): lax.all_to_all(copies, axis, 0, 0, axis_index_groups=groups, tiled=True)  8.55 us
  transfers between devices with their start and end apart: 23, of which 4 were waited for; matrix products, arithmetic and copies ran while one was open for 2% of the time, Pallas kernels for 20%

profile of v6, /device:TPU:112, one launch (start us, length us, event | category | flops | bytes accessed | tf_op | source)
XLA Modules:
  0.0 162.3 jit_solution(17416177884260373103)
XLA Ops:
  6.5 0.1 pad_add_fusion.where_ref
  6.6 1.7 %copy-done = bf16[768,1536]{1,0:T(8,128)(2,1)S(1)} copy-done((bf16[768,1536]{1,0:T(8,128)(2,1)S(1)}, bf16[768,1536]{1,0:T(8,128)(2,1)}, u32[]{:S(2)}) %copy-start) | copy-done | bytes 2359320
  8.3 1.7 %prepare.1 = (bf16[192,896]{1,0:T(8,128)(2,1)S(1)}, bf16[192,896]{1,0:T(8,128)(2,1)S(1)}, bf16[384,768]{1,0:T(8,128)(2,1)}, bf16[384,768]{1,0:T(8,128)(2,1)}) custom-call(s32[2]{0:T(128)S(1)} %pad_add_fusion.where_ref, bf16[768,1536]{1,0:T(8,128)(2,1)S(1)} %copy-done), custom_call_target="tpu_custom_call" | custom-call | tf_op jit(solution)/shard_map/prepare/pallas_call | solution.py:112
  10.0 0.7 collective-permute-start
  10.7 0.0 collective-permute-done
  10.7 0.1 add.61
  10.8 0.7 slice.57
  11.5 0.7 collective-permute-start.1
  12.1 0.7 collective-permute-start.4
  12.8 0.0 collective-permute-done.1
  12.9 0.2 broadcast_select_fusion
  13.1 0.0 copy-start.3
  13.1 0.1 fusion.2
  13.2 0.8 collective-permute-start.6
  14.0 0.7 collective-permute-start.8
  14.7 0.7 collective-permute-start.7
  15.5 0.7 collective-permute-start.2
  16.1 0.0 collective-permute-done.2
  16.2 0.7 collective-permute-start.3
  16.9 0.2 add.65
  17.1 0.7 collective-permute-start.5
  17.8 0.7 collective-permute-start.10
  18.6 0.1 fusion.1
  18.7 0.7 collective-permute-start.9
  19.5 0.7 collective-permute-start.11
  20.1 0.7 collective-permute-start.13
  20.8 1.3 collective-permute-start.12
  22.2 18.8 %collective-permute-done.12 = bf16[48,1536]{1,0:T(8,128)(2,1)S(1)} collective-permute-done((bf16[48,1536]{1,0:T(8,128)(2,1)S(1)}, bf16[48,1536]{1,0:T(8,128)(2,1)S(1)}, u32[]{:S(2)}, u32[]{:S(2)}) %collective-permute-start.12) | collective-permute-done | bytes 147488 | tf_op jit(solution)/shard_map/ppermute | solution.py:241
  41.1 1.3 collective-permute-start.16
  42.4 0.7 collective-permute-start.14
  43.1 0.7 collective-permute-start.15
  43.8 0.6 slice_select_fusion
  44.5 0.1 add.76
  44.6 1.3 collective-permute-start.18
  45.9 0.0 all-gather.2.cloned.1.call-update
  45.9 29.8 %collective-permute-done.18 = bf16[96,896]{1,0:T(8,128)(2,1)S(1)} collective-permute-done((bf16[96,896]{1,0:T(8,128)(2,1)S(1)}, bf16[96,896]{1,0:T(8,128)(2,1)S(1)}, u32[]{:S(2)}, u32[]{:S(2)}) %collective-permute-start.18) | collective-permute-done | bytes 172064 | tf_op jit(solution)/shard_map/ppermute | solution.py:241
  75.7 1.3 collective-permute-start.19
  77.0 1.0 collective-permute-done.19
  78.1 0.9 broadcast_in_dim.18
  79.0 3.5 %all-to-all-start.1 = ((bf16[4,96,896]{2,1,0:T(8,128)(2,1)}), bf16[4,96,896]{2,1,0:T(8,128)(2,1)S(1)}, u32[]{:S(2)}, u32[]{:S(2)}) async-start(bf16[4,96,896]{2,1,0:T(8,128)(2,1)} %broadcast_in_dim.18), calls=%async_computation.1 | async-start | bytes 1376256 | tf_op jit(solution)/shard_map/all_to_all | solution.py:273
  82.5 1.3 collective-permute-start.17
  83.8 22.4 %collective-permute-done.17 = bf16[192,768]{1,0:T(8,128)(2,1)S(1)} collective-permute-done((bf16[192,768]{1,0:T(8,128)(2,1)S(1)}, bf16[192,768]{1,0:T(8,128)(2,1)S(1)}, u32[]{:S(2)}, u32[]{:S(2)}) %collective-permute-start.17) | collective-permute-done | bytes 294944 | tf_op jit(solution)/shard_map/ppermute | solution.py:241
  106.2 0.1 add.78
  106.3 1.2 broadcast_in_dim.9
  107.4 5.1 %all-to-all-start = ((bf16[4,192,768]{2,1,0:T(8,128)(2,1)}), bf16[4,192,768]{2,1,0:T(8,128)(2,1)S(1)}, u32[]{:S(2)}, u32[]{:S(2)}) async-start(bf16[4,192,768]{2,1,0:T(8,128)(2,1)} %broadcast_in_dim.9), calls=%async_computation | async-start | bytes 2359296 | tf_op jit(solution)/shard_map/all_to_all | solution.py:273
  112.5 32.0 %factor.1 = (bf16[768,768]{1,0:T(8,128)(2,1)}, bf16[768,768]{1,0:T(8,128)(2,1)}) custom-call(bf16[384,896]{1,0:T(8,128)(2,1)} %bitcast.5), custom_call_target="tpu_custom_call" | custom-call | flops 40000000000 | bytes 4000000 | tf_op jit(solution)/shard_map/factor/pallas_call | solution.py:166
  144.5 0.0 all-gather.2.cloned.1.call-done.cols_ref
  144.6 10.9 %update.1 = bf16[768,1536]{1,0:T(8,128)(2,1)} custom-call(s32[2]{0:T(128)S(1)} %pad_add_fusion.where_ref, bf16[768,1536]{1,0:T(8,128)(2,1)} %cov_ref.3, bf16[768,768]{1,0:T(8,128)(2,1)S(1)} %bitcast.4, bf16[768,1536]{1,0:T(8,128)(2,1)} %all-gather.2.cloned.1.call-done.cols_ref, bf16[768,768]{1,0:T(8,128)(2,1)} %get-tuple-element.39.hi_ref, ...), custom_call_target="tpu_custom_call" | custom-call | tf_op jit(solution)/shard_map/update/pallas_call | solution.py:219
  (35 shorter events, 0.5 us)
Async XLA Ops:
  6.5 138.0 %all-gather.2.cloned.1.call-start = ((), (), s32[]{:S(2)}) async-start(), calls=%async_computation.2 | async-start | bytes 2433024 | tf_op jit(solution)/shard_map/all_gather | solution.py:315
  6.6 1.7 %copy-start = (bf16[768,1536]{1,0:T(8,128)(2,1)S(1)}, bf16[768,1536]{1,0:T(8,128)(2,1)}, u32[]{:S(2)}) copy-start(bf16[768,1536]{1,0:T(8,128)(2,1)} %cov_ref.3) | copy-start | bytes 7077892
  8.3 4.6 %copy-start.1 = (bf16[768,1536]{1,0:T(8,128)(2,1)S(1)}, bf16[768,1536]{1,0:T(8,128)(2,1)}, u32[]{:S(2)}) copy-start(bf16[768,1536]{1,0:T(8,128)(2,1)} %cov_ref.3) | copy-start | bytes 7077892
  10.0 0.7 collective-permute-start
  11.5 1.4 collective-permute-start.1
  12.1 4.7 %collective-permute-start.4 = (bf16[384,768]{1,0:T(8,128)(2,1)}, bf16[384,768]{1,0:T(8,128)(2,1)S(1)}, u32[]{:S(2)}, u32[]{:S(2)}) collective-permute-start(bf16[384,768]{1,0:T(8,128)(2,1)} %get-tuple-element.27), channel_id=1, source_target_pairs={{0,4},{16,20},{32,36},{48,52},{64,68},{80,84},{96,100},{112,116},{... | collective-permute-start | bytes 1769480 | tf_op jit(solution)/shard_map/ppermute | solution.py:241
  13.1 3.8 %copy-start.3 = (bf16[384,768]{1,0:T(8,128)(2,1)S(1)}, bf16[384,768]{1,0:T(8,128)(2,1)}, u32[]{:S(2)}) copy-start(bf16[384,768]{1,0:T(8,128)(2,1)} %get-tuple-element.26) | copy-start | bytes 1769476
  13.2 5.4 %collective-permute-start.6 = (bf16[192,1536]{1,0:T(8,128)(2,1)S(1)}, bf16[192,1536]{1,0:T(8,128)(2,1)S(1)}, u32[]{:S(2)}, u32[]{:S(2)}) collective-permute-start(bf16[192,1536]{1,0:T(8,128)(2,1)S(1)} %get-tuple-element.41), channel_id=1, source_target_pairs={{0,128},{1,129},{2,130},{3,131},{4,132},{5,133},{6,134},{7,135},{8... | collective-permute-start | bytes 1769480 | tf_op jit(solution)/shard_map/ppermute | solution.py:241
  14.0 4.6 %collective-permute-start.8 = (bf16[192,1536]{1,0:T(8,128)(2,1)S(1)}, bf16[192,1536]{1,0:T(8,128)(2,1)S(1)}, u32[]{:S(2)}, u32[]{:S(2)}) collective-permute-start(bf16[192,1536]{1,0:T(8,128)(2,1)S(1)} %get-tuple-element.42), channel_id=1, source_target_pairs={{0,384},{1,385},{2,386},{3,387},{4,388},{5,389},{6,390},{7,391},{8... | collective-permute-start | bytes 1769480 | tf_op jit(solution)/shard_map/ppermute | solution.py:241
  14.7 3.9 %collective-permute-start.7 = (bf16[192,1536]{1,0:T(8,128)(2,1)S(1)}, bf16[192,1536]{1,0:T(8,128)(2,1)S(1)}, u32[]{:S(2)}, u32[]{:S(2)}) collective-permute-start(bf16[192,1536]{1,0:T(8,128)(2,1)S(1)} %get-tuple-element.43), channel_id=1, source_target_pairs={{0,256},{1,257},{2,258},{3,259},{4,260},{5,261},{6,262},{7,263},{8... | collective-permute-start | bytes 1769480 | tf_op jit(solution)/shard_map/ppermute | solution.py:241
  15.5 0.7 collective-permute-start.2
  16.2 0.9 collective-permute-start.3
  17.1 1.4 collective-permute-start.5
  17.8 4.3 %collective-permute-start.10 = (bf16[192,768]{1,0:T(8,128)(2,1)S(1)}, bf16[192,768]{1,0:T(8,128)(2,1)S(1)}, u32[]{:S(2)}, u32[]{:S(2)}) collective-permute-start(bf16[192,768]{1,0:T(8,128)(2,1)S(1)} %slice.49), channel_id=1, source_target_pairs={{0,2},{16,18},{4,6},{20,22},{32,34},{48,50},{36,38},{52,54},{64,66... | collective-permute-start | bytes 884744 | tf_op jit(solution)/shard_map/ppermute | solution.py:241
  18.7 22.3 %collective-permute-start.9 = (bf16[96,896]{1,0:T(8,128)(2,1)S(1)}, bf16[96,896]{1,0:T(8,128)(2,1)S(1)}, u32[]{:S(2)}, u32[]{:S(2)}) collective-permute-start(bf16[96,896]{1,0:T(8,128)(2,1)S(1)} %add.66), channel_id=1, source_target_pairs={{0,4},{32,36},{64,68},{96,100},{8,12},{40,44},{72,76},{104,108},{1... | collective-permute-start | bytes 516104 | tf_op jit(solution)/shard_map/ppermute | solution.py:241
  19.5 2.7 %collective-permute-start.11 = (bf16[48,1536]{1,0:T(8,128)(2,1)S(1)}, bf16[48,1536]{1,0:T(8,128)(2,1)S(1)}, u32[]{:S(2)}, u32[]{:S(2)}) collective-permute-start(bf16[48,1536]{1,0:T(8,128)(2,1)S(1)} %get-tuple-element.44), channel_id=1, source_target_pairs={{0,32},{1,33},{2,34},{3,35},{4,36},{5,37},{6,38},{7,39},{8,40},{9,... | collective-permute-start | bytes 442376 | tf_op jit(solution)/shard_map/ppermute | solution.py:241
  20.1 2.0 %collective-permute-start.13 = (bf16[48,1536]{1,0:T(8,128)(2,1)S(1)}, bf16[48,1536]{1,0:T(8,128)(2,1)S(1)}, u32[]{:S(2)}, u32[]{:S(2)}) collective-permute-start(bf16[48,1536]{1,0:T(8,128)(2,1)S(1)} %get-tuple-element.45), channel_id=1, source_target_pairs={{0,96},{1,97},{2,98},{3,99},{4,100},{5,101},{6,102},{7,103},{8,104... | collective-permute-start | bytes 442376 | tf_op jit(solution)/shard_map/ppermute | solution.py:241
  20.8 20.2 %collective-permute-start.12 = (bf16[48,1536]{1,0:T(8,128)(2,1)S(1)}, bf16[48,1536]{1,0:T(8,128)(2,1)S(1)}, u32[]{:S(2)}, u32[]{:S(2)}) collective-permute-start(bf16[48,1536]{1,0:T(8,128)(2,1)S(1)} %get-tuple-element.46), channel_id=1, source_target_pairs={{0,64},{1,65},{2,66},{3,67},{4,68},{5,69},{6,70},{7,71},{8,72},{9,... | collective-permute-start | bytes 442376 | tf_op jit(solution)/shard_map/ppermute | solution.py:241
  41.1 2.7 %collective-permute-start.16 = (bf16[24,1536]{1,0:T(8,128)(2,1)S(1)}, bf16[24,1536]{1,0:T(8,128)(2,1)S(1)}, u32[]{:S(2)}, u32[]{:S(2)}) collective-permute-start(bf16[24,1536]{1,0:T(8,128)(2,1)S(1)} %slice.55), channel_id=1, source_target_pairs={{0,16},{32,48},{64,80},{96,112},{128,144},{160,176},{192,208},{224... | collective-permute-start | bytes 221192 | tf_op jit(solution)/shard_map/ppermute | solution.py:311
  42.4 2.0 %collective-permute-start.14 = (bf16[96,896]{1,0:T(8,128)(2,1)S(1)}, bf16[96,896]{1,0:T(8,128)(2,1)S(1)}, u32[]{:S(2)}, u32[]{:S(2)}) collective-permute-start(bf16[96,896]{1,0:T(8,128)(2,1)S(1)} %add.70), channel_id=1, source_target_pairs={{0,2},{4,6},{32,34},{36,38},{64,66},{68,70},{96,98},{100,102},{8,1... | collective-permute-start | bytes 516104 | tf_op jit(solution)/shard_map/ppermute | solution.py:241
  43.1 1.4 collective-permute-start.15
  44.6 31.1 %collective-permute-start.18 = (bf16[96,896]{1,0:T(8,128)(2,1)S(1)}, bf16[96,896]{1,0:T(8,128)(2,1)S(1)}, u32[]{:S(2)}, u32[]{:S(2)}) collective-permute-start(bf16[96,896]{1,0:T(8,128)(2,1)S(1)} %add.75), channel_id=1, source_target_pairs={{0,1},{2,3},{4,5},{6,7},{32,33},{34,35},{36,37},{38,39},{64,65},{6... | collective-permute-start | bytes 516104 | tf_op jit(solution)/shard_map/ppermute | solution.py:241
  75.7 2.3 %collective-permute-start.19 = (bf16[96,896]{1,0:T(8,128)(2,1)S(1)}, bf16[96,896]{1,0:T(8,128)(2,1)S(1)}, u32[]{:S(2)}, u32[]{:S(2)}) collective-permute-start(bf16[96,896]{1,0:T(8,128)(2,1)S(1)} %add.79), channel_id=1, source_target_pairs={{0,16},{32,48},{64,80},{96,112},{128,144},{160,176},{192,208},{224... | collective-permute-start | bytes 516104 | tf_op jit(solution)/shard_map/ppermute | solution.py:317
  79.0 27.3 %all-to-all-start.1 = ((bf16[4,96,896]{2,1,0:T(8,128)(2,1)}), bf16[4,96,896]{2,1,0:T(8,128)(2,1)S(1)}, u32[]{:S(2)}, u32[]{:S(2)}) async-start(bf16[4,96,896]{2,1,0:T(8,128)(2,1)} %broadcast_in_dim.18), calls=%async_computation.1 | async-start | bytes 1376256 | tf_op jit(solution)/shard_map/all_to_all | solution.py:273
  82.5 23.7 %collective-permute-start.17 = (bf16[192,768]{1,0:T(8,128)(2,1)S(1)}, bf16[192,768]{1,0:T(8,128)(2,1)S(1)}, u32[]{:S(2)}, u32[]{:S(2)}) collective-permute-start(bf16[192,768]{1,0:T(8,128)(2,1)S(1)} %add.76), channel_id=1, source_target_pairs={{0,8},{16,24},{1,9},{17,25},{2,10},{18,26},{3,11},{19,27},{4,12},{... | collective-permute-start | bytes 884744 | tf_op jit(solution)/shard_map/ppermute | solution.py:241
  106.3 6.3 %copy-start.2 = (bf16[4,96,896]{2,1,0:T(8,128)(2,1)}, bf16[4,96,896]{2,1,0:T(8,128)(2,1)S(1)}, u32[]{:S(2)}) copy-start(bf16[4,96,896]{2,1,0:T(8,128)(2,1)S(1)} %all-to-all-done.1) | copy-start | bytes 2064388
  107.4 37.1 %all-to-all-start = ((bf16[4,192,768]{2,1,0:T(8,128)(2,1)}), bf16[4,192,768]{2,1,0:T(8,128)(2,1)S(1)}, u32[]{:S(2)}, u32[]{:S(2)}) async-start(bf16[4,192,768]{2,1,0:T(8,128)(2,1)} %broadcast_in_dim.9), calls=%async_computation | async-start | bytes 2359296 | tf_op jit(solution)/shard_map/all_to_all | solution.py:273
Sparse Core Ops, SparseCore 0:
  46.0 87.9 all-gather.1
